TPU v7x, 32 devices: a whole 2x2x4 slice. The times are simulated.
32 devices in a mesh: grp: 2 (over y), tm: 8 (over z, x), tile: 2 (over core).
Axes of the slice: x: 2, y: 2, z: 4, core: 2. Of those that a mesh axis runs over, the one named last changes fastest.
Arguments:
- vis_data: float32 [4, 128, 4, 256], P(('grp', 'tile'), 'tm'), parts along dimension 0, may hold values from -6 to 6
- vis_weight: float32 [4, 128, 256], P(('grp', 'tile'), 'tm'), parts along dimension 0, may hold values from 0.2 to 5
- kernel_taps: float32 [4, 128, 2, 8, 256], P(('grp', 'tile'), 'tm'), parts along dimension 0, may hold values from 0.2 to 1
- offsets: int32 [4, 128, 2, 256], P(('grp', 'tile'), 'tm'), parts along dimension 0, may hold values from 0 to 120
- block_patch: int32 [4, 128], P(('grp', 'tile'), 'tm'), parts along dimension 0, may hold values from 0 to 7
- block_count: int32 [4, 8], P(('grp', 'tile'), 'tm'), parts along dimension 0, may hold values from 1 to 16, 64 in all within a row
Outputs:
- image: float32 [2, 2, 8, 256, 256], P(None, None, ('grp', 'tile'), 'tm'), parts along dimension 2
There are 2 independent parts, one for each index of `grp`. A program takes and returns all parts, laid end to end along the dimension named above; each array names one. Nothing has to cross between parts.
Inputs may be any that keep to these rules, and one draw needn't show every extreme that they name: Each row of block_count sums to 64, and its largest entry is 16 in every draw.
All inputs are finite; a program needn't handle non-finite values.
Results may differ from a plain program's by a relative error of at most 0.0037.
Values sent between devices are 32-bit elements; how exact they have to be, the bound alone decides.
No kernel may reach another device: no remote copies, remote signals or barrier semaphores. Data moves between devices by JAX's collectives and lax.ppermute only.
A program may use at most 64 MiB of HBM per device.

v0:
```python
import math

import jax
import jax.numpy as jnp
import ml_dtypes
import numpy as np
from jax import lax
from jax.experimental import pallas as pl
from jax.experimental.pallas import tpu as pltpu
from jax.sharding import PartitionSpec as P

G = 256
P_SIZE = 128
K = 8
B = 256
POLS = 2
NT_C = 2
PATCHES = 4 * NT_C
GRIDS = 1 + 2 * POLS
LANES = 128
HALVES = B // LANES
AUX = GRIDS + 2
TAP_ROWS = 2 * HALVES * K
ID_START = TAP_ROWS + AUX * HALVES
PIECE_ROWS = ID_START + 1
HIGH = lax.Precision.HIGHEST
VMEM = pl.BlockSpec(memory_space=pltpu.VMEM)
PARAMS = pltpu.CompilerParams(vmem_limit_bytes=20 * 1024 * 1024)


def half_lanes(half):
    return slice(half * LANES, (half + 1) * LANES)


def pack_kernel(pieces, vis_hbm, weight_hbm, taps_hbm, offs_hbm, patch_hbm, count_ref, *refs):
    outs, scratch = refs[: len(pieces)], refs[len(pieces) :]
    vis_ref, weight_ref, taps_ref, offs_ref, patch_ref, sems = scratch
    pairs = (
        (offs_hbm, offs_ref),
        (taps_hbm, taps_ref),
        (weight_hbm, weight_ref),
        (vis_hbm, vis_ref),
        (patch_hbm, patch_ref),
    )
    copies = [pltpu.make_async_copy(a, b, sems.at[i]) for i, (a, b) in enumerate(pairs)]
    for copy in copies:
        copy.start()
    bases = [sum(pieces[:i]) for i in range(len(pieces))]
    copies[0].wait()
    copies[1].wait()
    for out_ref, n, base in zip(outs, pieces, bases):
        for j in range(n):
            for side in range(2):
                off = offs_ref[base + j, side : side + 1, :]
                taps = taps_ref[base + j, side]
                for bit in range(3):
                    moved = pltpu.roll(taps, 1 << bit, 0)
                    turn = jnp.broadcast_to((off >> bit) & 1, taps.shape) == 1
                    taps = jnp.where(turn, moved, taps)
                for half in range(HALVES):
                    at = j * TAP_ROWS + (side * HALVES + half) * K
                    out_ref[at : at + K, :] = taps[:, half_lanes(half)]
    copies[2].wait()
    copies[3].wait()
    copies[4].wait()
    for out_ref, n, base in zip(outs, pieces, bases):
        for half in range(HALVES):
            lanes = half_lanes(half)
            weight = weight_ref[base : base + n, lanes]
            kinds = [weight] + [weight * vis_ref[base : base + n, m, lanes] for m in range(2 * POLS)]
            kinds += [offs_ref[base : base + n, side, lanes].astype(jnp.float32) for side in range(2)]
            for kind, rows in enumerate(kinds):
                at = n * (TAP_ROWS + kind * HALVES + half)
                out_ref[at : at + n, :] = rows
        for j in range(n):
            patch = jnp.where(base + j < count_ref[0, 0], patch_ref[0, base + j], -1)
            row = jnp.full((1, LANES), patch, jnp.int32).astype(jnp.float32)
            out_ref[n * ID_START + j : n * ID_START + j + 1, :] = row


def pack(pieces, vis, weight, taps, offs, patches, count):
    arrays = (vis, weight, taps, offs, patches)
    spaces = [pltpu.VMEM] * 4 + [pltpu.SMEM]
    hbm, smem = pl.BlockSpec(memory_space=pltpu.HBM), pl.BlockSpec(memory_space=pltpu.SMEM)
    return pl.pallas_call(
        lambda *refs: pack_kernel(pieces, *refs),
        out_shape=[jax.ShapeDtypeStruct((n * PIECE_ROWS, LANES), jnp.float32) for n in pieces],
        in_specs=[hbm] * 5 + [smem],
        out_specs=[VMEM] * len(pieces),
        scratch_shapes=[space(a.shape, a.dtype) for space, a in zip(spaces, arrays)] + [pltpu.SemaphoreType.DMA((5,))],
        compiler_params=PARAMS,
        name="pack",
    )(*[pltpu.with_memory_space_constraint(a, pltpu.HBM) for a in arrays], count)


def spread(off):
    row = lax.broadcasted_iota(jnp.int32, (16, B), 0)
    gap = off.astype(jnp.int32) - row
    step = (gap + 15) >> 4
    inside = (step << 4) - gap < K
    return jnp.where(inside, step, -1).astype(jnp.float32).astype(jnp.bfloat16)


def slot_taps(buf_ref, j, side):
    starts = [j * TAP_ROWS + (side * HALVES + half) * K for half in range(HALVES)]
    rows = jnp.concatenate([buf_ref[at : at + K, :] for at in starts], axis=1)
    return jnp.concatenate([rows, rows], axis=0)


def slot_row(buf_ref, n, j, kind):
    starts = [n * (TAP_ROWS + kind * HALVES + half) + j for half in range(HALVES)]
    return jnp.concatenate([buf_ref[at : at + 1, :] for at in starts], axis=1)


def slot_patch(buf_ref, n, j):
    return buf_ref[n * ID_START + j : n * ID_START + j + 1, 0:1][0, 0].astype(jnp.int32)


def block_factors(buf_ref, n, j, live, grids):
    rows_u = slot_taps(buf_ref, j, 0)
    rows_v = slot_taps(buf_ref, j, 1)
    step_u = spread(slot_row(buf_ref, n, j, GRIDS))
    step_v = spread(slot_row(buf_ref, n, j, GRIDS + 1))
    if live is not None:
        rows_v = jnp.where(live, rows_v, 0.0)
    rows_v = rows_v.astype(jnp.bfloat16)
    zero = jnp.zeros((16, B), jnp.bfloat16)
    steps = P_SIZE // 16
    right = jnp.concatenate([jnp.where(step_v == s, rows_v, zero) for s in range(steps)], axis=0)
    hits = [step_u == s for s in range(steps)]
    left = []
    for e in grids:
        product = (rows_u * slot_row(buf_ref, n, j, e)).astype(jnp.bfloat16)
        left += [jnp.where(hit, product, zero) for hit in hits]
    return jnp.concatenate(left, axis=0), right


def add_some(buf_ref, acc_ref, n, slots, grids):
    lanes = slice(grids[0] * P_SIZE, (grids[-1] + 1) * P_SIZE)
    waiting = None
    for i, j in enumerate(slots):
        where_at = slot_patch(buf_ref, n, j)
        left, right = block_factors(buf_ref, n, j, where_at >= 0 if i else None, grids)
        patch = lax.dot_general(
            right, left, (((1,), (1,)), ((), ())), preferred_element_type=jnp.float32
        )
        if waiting is not None:
            acc_ref[waiting[0], :, lanes] += waiting[1]
        waiting = jnp.maximum(where_at, 0), patch
    acc_ref[waiting[0], :, lanes] += waiting[1]


def grid_kernel(n_bufs, first, last, grids, *refs):
    acc_ref = refs[n_bufs] if first else refs[n_bufs + 1]
    if first:
        acc_ref[...] = jnp.zeros_like(acc_ref)
    for buf_ref in refs[:n_bufs]:
        n = buf_ref.shape[0] // PIECE_ROWS
        for low in range(0, n, 8):
            few, many = range(low, min(low + 4, n)), range(low, min(low + 8, n))
            some = slot_patch(buf_ref, n, low) >= 0
            more = slot_patch(buf_ref, n, low + 4) >= 0 if len(many) > 4 else jnp.bool_(False)

            @pl.when(more)
            def _(buf_ref=buf_ref, n=n, many=many):
                add_some(buf_ref, acc_ref, n, many, grids)

            @pl.when(jnp.logical_and(some, jnp.logical_not(more)))
            def _(buf_ref=buf_ref, n=n, few=few):
                add_some(buf_ref, acc_ref, n, few, grids)

    if last:
        sums_ref = refs[-1]
        dens = acc_ref[:, :, :P_SIZE]
        for i, value in enumerate((dens, dens * dens)):
            part = jnp.sum(value.reshape(-1, 8, P_SIZE), axis=0)
            part = jnp.sum(jnp.sum(part, axis=0, keepdims=True), axis=1, keepdims=True)
            sums_ref[8 * i : 8 * i + 8, :] = jnp.broadcast_to(part, (8, P_SIZE))


def add_blocks(acc, bufs, last=False, grids=range(GRIDS)):
    first = acc is None
    n = len(bufs)
    slots = sum(buf.shape[0] for buf in bufs) // PIECE_ROWS
    out_shape = [jax.ShapeDtypeStruct((PATCHES, P_SIZE, GRIDS * P_SIZE), jnp.float32)]
    if last:
        out_shape.append(jax.ShapeDtypeStruct((16, P_SIZE), jnp.float32))
    args = list(bufs) + ([] if first else [acc])
    flops = (2 if first else 4) * slots * len(grids) * P_SIZE * P_SIZE * B
    out = pl.pallas_call(
        lambda *refs: grid_kernel(n, first, last, grids, *refs),
        out_shape=out_shape,
        in_specs=[VMEM] * len(args),
        out_specs=[VMEM] * len(out_shape),
        input_output_aliases={} if first else {n: 0},
        compiler_params=PARAMS,
        cost_estimate=pl.CostEstimate(flops=flops, bytes_accessed=slots * PIECE_ROWS * LANES, transcendentals=0),
        name="grid",
    )(*args)
    return tuple(out) if last else out[0]


def two_parts(value):
    high = value.astype(jnp.bfloat16)
    return high, (value - high.astype(jnp.float32)).astype(jnp.bfloat16)


def image_kernel(acc_ref, mine_ref, other_ref, row_ref, col_ref, out_ref):
    s1 = mine_ref[0:1, :] + other_ref[0:1, :]
    s2 = mine_ref[8:9, :] + other_ref[8:9, :]
    factor = 2.5 * s1 / s2
    width = out_ref.shape[3]
    half = 2 * width
    done = []
    for t in range(NT_C):
        tiles = [[acc_ref.at[4 * t + 2 * pr + pc] for pr in range(2)] for pc in range(2)]
        weights = [[1.0 / (1.0 + factor * tile[:, :P_SIZE]) for tile in pair] for pair in tiles]
        for pol in range(POLS):
            cells = []
            for e in (1 + 2 * pol, 2 + 2 * pol):
                for pc in range(2):
                    strip = [
                        tiles[pc][pr][:, e * P_SIZE : (e + 1) * P_SIZE] * weights[pc][pr] for pr in range(2)
                    ]
                    cells.append(jnp.concatenate(strip, axis=1))
            high, low = two_parts(jnp.concatenate(cells, axis=0))
            both = jnp.dot(row_ref[...], high, preferred_element_type=jnp.float32)
            rest = jnp.dot(row_ref[:half], low, preferred_element_type=jnp.float32)
            done.append(both[:half] + both[half:] + rest)
    high, low = two_parts(jnp.concatenate(done, axis=0))
    both = jnp.dot(high, col_ref[...], preferred_element_type=jnp.float32)
    rest = jnp.dot(low, col_ref[:, : 2 * G], preferred_element_type=jnp.float32)
    done = both[:, : 2 * G] + both[:, 2 * G :] + rest
    for t in range(NT_C):
        for pol in range(POLS):
            at = (t * POLS + pol) * half
            real, imag = done[at : at + width], done[at + width : at + half]
            out_ref[pol, 0, t] = real[:, :G] + imag[:, G:]
            out_ref[pol, 1, t] = imag[:, :G] - real[:, G:]


def make_image(acc, mine, other, row_table, col_table, width):
    return pl.pallas_call(
        image_kernel,
        out_shape=jax.ShapeDtypeStruct((POLS, 2, NT_C, width, G), jnp.float32),
        in_specs=[VMEM] * 5,
        out_specs=VMEM,
        compiler_params=PARAMS,
        name="image",
    )(acc, mine, other, row_table, col_table)


def dft_tables():
    index = np.arange(G)
    phase = (index[:, None] * index[None, :] % G) * (2.0 * math.pi / G)
    return np.cos(phase).astype(np.float32), np.sin(phase).astype(np.float32)


def np_parts(table, axis):
    high = table.astype(ml_dtypes.bfloat16)
    low = (table - high.astype(np.float32)).astype(ml_dtypes.bfloat16)
    return np.concatenate([high, low], axis=axis)


def image_tables(n_tm):
    cosine, sine = dft_tables()
    rows = []
    for cos_part, sin_part in zip(np.split(cosine, n_tm, axis=1), np.split(sine, n_tm, axis=1)):
        rows.append(np_parts(np.block([[cos_part, -sin_part], [sin_part, cos_part]]).T, 0))
    return np.stack(rows), np_parts(np.concatenate([cosine, sine], axis=1) / G, 1)


def by_gather(packed, n_tm, n_tile):
    order = list(range(0, n_tm, 2)) + list(range(1, n_tm, 2))[::-1]
    ways = [[], []]
    for i in range(n_tm):
        for tile in range(n_tile):
            here, there = (n_tile * order[k] + tile for k in (i, (i + 1) % n_tm))
            ways[tile % 2].append((here, there))
            ways[1 - tile % 2].append((there, here))

    def both_ways(pair):
        return [lax.ppermute(a, ("tm", "tile"), way) for a, way in zip(pair, ways)]

    leading = both_ways(packed)
    trailing = both_ways(packed[::-1])
    acc = add_blocks(None, packed)
    for step in range(2, n_tm // 2 + 1):
        following = both_ways(leading)
        acc = add_blocks(acc, leading)
        acc, *trailing = lax.optimization_barrier((acc, *trailing))
        leading = following
        following = both_ways(trailing) if step < n_tm // 2 else None
        acc = add_blocks(acc, trailing)
        trailing = following
    acc = add_blocks(acc, leading[:1], grids=range(1))
    acc, sums = add_blocks(acc, leading[1:], last=True, grids=range(1))
    return add_blocks(acc, leading, grids=range(1, GRIDS)), sums


def rest_by_rows(acc, cosine, sine):
    grid = acc.reshape(NT_C, 2, 2, P_SIZE, GRIDS, P_SIZE)
    flat = jnp.transpose(grid, (4, 0, 1, 5, 2, 3)).reshape(GRIDS, NT_C * G, G)
    owned = lax.psum_scatter(flat, "tm", scatter_dimension=1, tiled=True)
    dens = owned[0]
    totals = lax.psum((jnp.sum(dens), jnp.sum(dens * dens)), ("tm", "tile"))
    factor = 2.5 * totals[0] / totals[1]
    weighted = owned[1:] / (1.0 + factor * dens[None])
    weighted = weighted.reshape(POLS, 2, dens.shape[0], G)
    real, imag = weighted[:, 0], weighted[:, 1]

    def rows(a, b):
        return jnp.einsum("prj,jn->prn", a, b, precision=HIGH)

    done = jnp.stack([rows(real, cosine) + rows(imag, sine), rows(imag, cosine) - rows(real, sine)], axis=1)
    width = G // lax.axis_size("tm")
    every_row = lax.all_gather(done, "tm", axis=2, tiled=True)
    columns = lax.dynamic_slice_in_dim(every_row, lax.axis_index("tm") * width, width, 3)
    columns = columns.reshape(POLS, 2, NT_C, G, width)
    real, imag = columns[:, 0], columns[:, 1]

    def cols(a, b):
        return jnp.einsum("mi,ptic->ptcm", a, b, precision=HIGH)

    out = jnp.stack([cols(cosine, real) + cols(sine, imag), cols(cosine, imag) - cols(sine, real)], axis=1)
    return out / G


def body(vis_data, vis_weight, kernel_taps, offsets, block_patch, block_count):
    slots = vis_weight.shape[1]
    n_tm = lax.axis_size("tm")
    pieces = (slots // 2, slots - slots // 2)
    packed = pack(pieces, vis_data[0], vis_weight[0], kernel_taps[0], offsets[0], block_patch, block_count)
    if n_tm > 8:
        cosine, sine = dft_tables()
        return rest_by_rows(add_blocks(None, packed), jnp.asarray(cosine), jnp.asarray(sine))
    n_tile = lax.axis_size("tile")
    acc, mine = by_gather(packed, n_tm, n_tile)
    other = lax.ppermute(mine, "tile", [(i, n_tile - 1 - i) for i in range(n_tile)])
    row_tables, col_table = image_tables(n_tm)
    row_table = lax.dynamic_index_in_dim(jnp.asarray(row_tables), lax.axis_index("tm"), 0, keepdims=False)
    return make_image(acc, mine, other, row_table, jnp.asarray(col_table), G // n_tm)


def solution(mesh):
    return jax.shard_map(
        body,
        mesh=mesh,
        in_specs=(
            P(("grp", "tile"), "tm", None, None),
            P(("grp", "tile"), "tm", None),
            P(("grp", "tile"), "tm", None, None, None),
            P(("grp", "tile"), "tm", None, None),
            P(("grp", "tile"), "tm"),
            P(("grp", "tile"), "tm"),
        ),
        out_specs=P(None, None, ("grp", "tile"), "tm", None),
        check_vma=False,
    )
```

profile of v0, /device:TPU:1, one launch (start us, length us, event | category | flops | bytes accessed | tf_op | source)
XLA Modules:
  0.0 39.2 jit_solution(13769084622208477022)
XLA Ops:
  0.7 1.2 %pack.1 = (f32[376,128]{1,0:T(8,128)S(1)}, f32[376,128]{1,0:T(8,128)S(1)}) custom-call(f32[16,4,256]{2,1,0:T(4,128)} %bitcast.7, f32[16,256]{1,0:T(8,128)} %bitcast.9, f32[16,2,8,256]{3,2,1,0:T(8,128)} %bitcast.6, s32[16,2,256]{2,1,0:T(2,128)} %bitcast.8, s32[1,16]{1,0:T(1,128)} %refs_4_.1, s32[1,1]{1,0:T(1,128)S(6)} %copy.27.refs_5_), custom_call_target="tpu_custom_call" | custom-call | tf_op jit(solution)/shard_map/pack/pallas_call | solution.py:85
  1.9 2.1 %collective-permute-start = (f32[376,128]{1,0:T(8,128)S(1)}, f32[376,128]{1,0:T(8,128)S(1)}, u32[]{:S(2)}, u32[]{:S(2)}) collective-permute-start(f32[376,128]{1,0:T(8,128)S(1)} %get-tuple-element.18.refs_0_), channel_id=1, source_target_pairs={{0,4},{5,1},{4,8},{9,5},{8,12},{13,9},{12,14},{15,13},{14,10},{11,... | collective-permute-start | bytes 577544 | tf_op jit(solution)/shard_map/ppermute | solution.py:283
  4.0 0.2 collective-permute-start.4
  4.1 1.3 %collective-permute-start.8 = (f32[376,128]{1,0:T(8,128)S(1)}, f32[376,128]{1,0:T(8,128)S(1)}, u32[]{:S(2)}, u32[]{:S(2)}) collective-permute-start(f32[376,128]{1,0:T(8,128)S(1)} %get-tuple-element.19.refs_1_), channel_id=1, source_target_pairs={{0,4},{5,1},{4,8},{9,5},{8,12},{13,9},{12,14},{15,13},{14,10},{11,... | collective-permute-start | bytes 577544 | tf_op jit(solution)/shard_map/ppermute | solution.py:283
  5.5 0.2 collective-permute-start.9
  5.6 0.9 %dynamic-slice_bitcast_fusion.row_ref = bf16[128,512]{1,0:T(8,128)(2,1)S(1)} fusion(bf16[8,128,512]{2,1,0:T(8,128)(2,1)} %constant.16.clone, s32[]{:T(128)S(6)} %select_n.4), kind=kLoop, calls=%fused_computation | loop fusion | bytes 262148 | tf_op jit(solution)/shard_map/jit(dynamic_index_in_dim)/squeeze | solution.py:341
  6.5 0.8 %grid.10.refs_2_ = f32[8,128,640]{2,1,0:T(8,128)S(1)} custom-call(f32[376,128]{1,0:T(8,128)S(1)} %get-tuple-element.18.refs_0_, f32[376,128]{1,0:T(8,128)S(1)} %get-tuple-element.19.refs_1_), custom_call_target="tpu_custom_call" | custom-call | flops 671088640 | bytes 96256 | tf_op jit(solution)/shard_map/grid/pallas_call | solution.py:190
  7.4 0.0 collective-permute-done.refs_0_
  7.4 2.7 %collective-permute-start.1 = (f32[376,128]{1,0:T(8,128)S(1)}, f32[376,128]{1,0:T(8,128)S(1)}, u32[]{:S(2)}, u32[]{:S(2)}) collective-permute-start(f32[376,128]{1,0:T(8,128)S(1)} %collective-permute-done.refs_0_), channel_id=1, source_target_pairs={{0,4},{5,1},{4,8},{9,5},{8,12},{13,9},{12,14},{15,13},{14,10},{11,... | collective-permute-start | bytes 577544 | tf_op jit(solution)/shard_map/ppermute | solution.py:283
  10.1 0.6 %collective-permute-done.4.refs_1_ = f32[376,128]{1,0:T(8,128)S(1)} collective-permute-done((f32[376,128]{1,0:T(8,128)S(1)}, f32[376,128]{1,0:T(8,128)S(1)}, u32[]{:S(2)}, u32[]{:S(2)}) %collective-permute-start.4) | collective-permute-done | bytes 192544 | tf_op jit(solution)/shard_map/ppermute | solution.py:283
  10.8 0.0 collective-permute-start.5
  10.8 1.6 %grid.11.refs_2_ = f32[8,128,640]{2,1,0:T(8,128)S(1)} custom-call(f32[376,128]{1,0:T(8,128)S(1)} %collective-permute-done.refs_0_, f32[376,128]{1,0:T(8,128)S(1)} %collective-permute-done.4.refs_1_, f32[8,128,640]{2,1,0:T(8,128)S(1)} %grid.10.refs_2_), custom_call_target="tpu_custom_call", output_to_operand_aliasing={{}: (2, {})} | custom-call | flops 1342177280 | bytes 96256 | tf_op jit(solution)/shard_map/grid/pallas_call | solution.py:190
  12.4 0.0 collective-permute-done.8.refs_0_
  12.4 2.5 %collective-permute-done.9.refs_1_ = f32[376,128]{1,0:T(8,128)S(1)} collective-permute-done((f32[376,128]{1,0:T(8,128)S(1)}, f32[376,128]{1,0:T(8,128)S(1)}, u32[]{:S(2)}, u32[]{:S(2)}) %collective-permute-start.9) | collective-permute-done | bytes 192544 | tf_op jit(solution)/shard_map/ppermute | solution.py:283
  14.9 1.4 %collective-permute-start.10 = (f32[376,128]{1,0:T(8,128)S(1)}, f32[376,128]{1,0:T(8,128)S(1)}, u32[]{:S(2)}, u32[]{:S(2)}) collective-permute-start(f32[376,128]{1,0:T(8,128)S(1)} %collective-permute-done.8.refs_0_), channel_id=1, source_target_pairs={{0,4},{5,1},{4,8},{9,5},{8,12},{13,9},{12,14},{15,13},{14,10},{11,... | collective-permute-start | bytes 577544 | tf_op jit(solution)/shard_map/ppermute | solution.py:283
  16.2 0.1 collective-permute-start.11
  16.4 1.1 %grid.12.refs_2_ = f32[8,128,640]{2,1,0:T(8,128)S(1)} custom-call(f32[376,128]{1,0:T(8,128)S(1)} %collective-permute-done.8.refs_0_, f32[376,128]{1,0:T(8,128)S(1)} %collective-permute-done.9.refs_1_, f32[8,128,640]{2,1,0:T(8,128)S(1)} %grid.11.refs_2_), custom_call_target="tpu_custom_call", output_to_operand_aliasing={{}: (2, {})} | custom-call | flops 1342177280 | bytes 96256 | tf_op jit(solution)/shard_map/grid/pallas_call | solution.py:190
  17.4 0.0 collective-permute-done.1.refs_0_
  17.4 1.4 %collective-permute-start.2 = (f32[376,128]{1,0:T(8,128)S(1)}, f32[376,128]{1,0:T(8,128)S(1)}, u32[]{:S(2)}, u32[]{:S(2)}) collective-permute-start(f32[376,128]{1,0:T(8,128)S(1)} %collective-permute-done.1.refs_0_), channel_id=1, source_target_pairs={{0,4},{5,1},{4,8},{9,5},{8,12},{13,9},{12,14},{15,13},{14,10},{11,... | collective-permute-start | bytes 577544 | tf_op jit(solution)/shard_map/ppermute | solution.py:283
  18.9 0.0 collective-permute-done.5.refs_1_
  18.9 0.1 collective-permute-start.6
  19.0 1.1 %grid.13.refs_2_ = f32[8,128,640]{2,1,0:T(8,128)S(1)} custom-call(f32[376,128]{1,0:T(8,128)S(1)} %collective-permute-done.1.refs_0_, f32[376,128]{1,0:T(8,128)S(1)} %collective-permute-done.5.refs_1_, f32[8,128,640]{2,1,0:T(8,128)S(1)} %grid.12.refs_2_), custom_call_target="tpu_custom_call", output_to_operand_aliasing={{}: (2, {})} | custom-call | flops 1342177280 | bytes 96256 | tf_op jit(solution)/shard_map/grid/pallas_call | solution.py:190
  20.0 0.0 collective-permute-done.10.refs_0_
  20.1 2.7 %collective-permute-done.11.refs_1_ = f32[376,128]{1,0:T(8,128)S(1)} collective-permute-done((f32[376,128]{1,0:T(8,128)S(1)}, f32[376,128]{1,0:T(8,128)S(1)}, u32[]{:S(2)}, u32[]{:S(2)}) %collective-permute-start.11) | collective-permute-done | bytes 192544 | tf_op jit(solution)/shard_map/ppermute | solution.py:283
  22.8 1.7 %collective-permute-start.12 = (f32[376,128]{1,0:T(8,128)S(1)}, f32[376,128]{1,0:T(8,128)S(1)}, u32[]{:S(2)}, u32[]{:S(2)}) collective-permute-start(f32[376,128]{1,0:T(8,128)S(1)} %collective-permute-done.10.refs_0_), channel_id=1, source_target_pairs={{0,4},{5,1},{4,8},{9,5},{8,12},{13,9},{12,14},{15,13},{14,10},{11,... | collective-permute-start | bytes 577544 | tf_op jit(solution)/shard_map/ppermute | solution.py:283
  24.5 0.0 collective-permute-start.13
  24.5 1.8 %grid.14.refs_2_ = f32[8,128,640]{2,1,0:T(8,128)S(1)} custom-call(f32[376,128]{1,0:T(8,128)S(1)} %collective-permute-done.10.refs_0_, f32[376,128]{1,0:T(8,128)S(1)} %collective-permute-done.11.refs_1_, f32[8,128,640]{2,1,0:T(8,128)S(1)} %grid.13.refs_2_), custom_call_target="tpu_custom_call", output_to_operand_aliasing={{}: (2, {})} | custom-call | flops 1342177280 | bytes 96256 | tf_op jit(solution)/shard_map/grid/pallas_call | solution.py:190
  26.3 0.0 collective-permute-done.2.refs_0_
  26.3 0.5 %collective-permute-start.3 = (f32[376,128]{1,0:T(8,128)S(1)}, f32[376,128]{1,0:T(8,128)S(1)}, u32[]{:S(2)}, u32[]{:S(2)}) collective-permute-start(f32[376,128]{1,0:T(8,128)S(1)} %collective-permute-done.2.refs_0_), channel_id=1, source_target_pairs={{0,4},{5,1},{4,8},{9,5},{8,12},{13,9},{12,14},{15,13},{14,10},{11,... | collective-permute-start | bytes 577544 | tf_op jit(solution)/shard_map/ppermute | solution.py:283
  26.9 0.1 collective-permute-done.6.refs_1_
  27.0 0.9 %collective-permute-start.7 = (f32[376,128]{1,0:T(8,128)S(1)}, f32[376,128]{1,0:T(8,128)S(1)}, u32[]{:S(2)}, u32[]{:S(2)}) collective-permute-start(f32[376,128]{1,0:T(8,128)S(1)} %collective-permute-done.6.refs_1_), channel_id=1, source_target_pairs={{4,0},{1,5},{8,4},{5,9},{12,8},{9,13},{14,12},{13,15},{10,14},{15,... | collective-permute-start | bytes 577544 | tf_op jit(solution)/shard_map/ppermute | solution.py:283
  27.8 1.1 %grid.15.refs_2_ = f32[8,128,640]{2,1,0:T(8,128)S(1)} custom-call(f32[376,128]{1,0:T(8,128)S(1)} %collective-permute-done.2.refs_0_, f32[376,128]{1,0:T(8,128)S(1)} %collective-permute-done.6.refs_1_, f32[8,128,640]{2,1,0:T(8,128)S(1)} %grid.14.refs_2_), custom_call_target="tpu_custom_call", output_to_operand_aliasing={{}: (2, {})} | custom-call | flops 1342177280 | bytes 96256 | tf_op jit(solution)/shard_map/grid/pallas_call | solution.py:190
  28.9 0.0 collective-permute-done.12.refs_0_
  28.9 1.7 %collective-permute-done.13.refs_1_ = f32[376,128]{1,0:T(8,128)S(1)} collective-permute-done((f32[376,128]{1,0:T(8,128)S(1)}, f32[376,128]{1,0:T(8,128)S(1)}, u32[]{:S(2)}, u32[]{:S(2)}) %collective-permute-start.13) | collective-permute-done | bytes 192544 | tf_op jit(solution)/shard_map/ppermute | solution.py:283
  30.7 1.6 %grid.16.refs_1_ = f32[8,128,640]{2,1,0:T(8,128)S(1)} custom-call(f32[376,128]{1,0:T(8,128)S(1)} %collective-permute-done.12.refs_0_, f32[376,128]{1,0:T(8,128)S(1)} %collective-permute-done.13.refs_1_, f32[8,128,640]{2,1,0:T(8,128)S(1)} %grid.15.refs_2_), custom_call_target="tpu_custom_call", output_to_operand_aliasing={{}: (2, {})} | custom-call | flops 1342177280 | bytes 96256 | tf_op jit(solution)/shard_map/grid/pallas_call | solution.py:190
  32.3 0.0 collective-permute-done.3.refs_0_
  32.4 0.4 %grid.17.refs_1_ = f32[8,128,640]{2,1,0:T(8,128)S(1)} custom-call(f32[376,128]{1,0:T(8,128)S(1)} %collective-permute-done.3.refs_0_, f32[8,128,640]{2,1,0:T(8,128)S(1)} %grid.16.refs_1_), custom_call_target="tpu_custom_call", output_to_operand_aliasing={{}: (1, {})} | custom-call | flops 134217728 | bytes 48128 | tf_op jit(solution)/shard_map/grid/pallas_call | solution.py:190
  32.8 2.0 %collective-permute-done.7.refs_0_.refs_1_ = f32[376,128]{1,0:T(8,128)S(1)} collective-permute-done((f32[376,128]{1,0:T(8,128)S(1)}, f32[376,128]{1,0:T(8,128)S(1)}, u32[]{:S(2)}, u32[]{:S(2)}) %collective-permute-start.7) | collective-permute-done | bytes 192544 | tf_op jit(solution)/shard_map/ppermute | solution.py:283
  34.8 0.3 grid.18
  35.1 1.5 %collective-permute-start.14 = (f32[16,128]{1,0:T(8,128)S(1)}, f32[16,128]{1,0:T(8,128)S(1)}, u32[]{:S(2)}, u32[]{:S(2)}) collective-permute-start(f32[16,128]{1,0:T(8,128)S(1)} %get-tuple-element.30.mine_ref), channel_id=1, source_target_pairs={{0,1},{1,0},{2,3},{3,2},{4,5},{5,4},{6,7},{7,6},{8,9},{9,8},{10,11... | collective-permute-start | bytes 24584 | tf_op jit(solution)/shard_map/ppermute | solution.py:339
  36.6 0.0 copy-start
  36.6 0.9 %grid.19.acc_ref = f32[8,128,640]{2,1,0:T(8,128)S(1)} custom-call(f32[376,128]{1,0:T(8,128)S(1)} %collective-permute-done.3.refs_0_, f32[376,128]{1,0:T(8,128)S(1)} %collective-permute-done.7.refs_0_.refs_1_, f32[8,128,640]{2,1,0:T(8,128)S(1)} %get-tuple-element.29.refs_2_), custom_call_target="tpu_custom_call", output_to_operand_aliasing={{}: (2, {})} | custom-call | flops 1073741824 | bytes 96256 | tf_op jit(solution)/shard_map/grid/pallas_call | solution.py:190
  37.5 0.0 collective-permute-done.14.other_ref
  37.6 0.1 copy-done
  37.6 1.6 %image.1 = f32[2,2,2,32,256]{4,3,2,1,0:T(8,128)} custom-call(f32[8,128,640]{2,1,0:T(8,128)S(1)} %grid.19.acc_ref, f32[16,128]{1,0:T(8,128)S(1)} %get-tuple-element.30.mine_ref, f32[16,128]{1,0:T(8,128)S(1)} %collective-permute-done.14.other_ref, bf16[128,512]{1,0:T(8,128)(2,1)S(1)} %dynamic-slice_bitcast_fusion.row_ref, bf16[256,1024]{1,0:T(8,128)(2,1)S(1)} %copy-done), custom_call_target="tpu_custom_call" | custom-call | tf_op jit(solution)/shard_map/image/pallas_call | solution.py:243
Async XLA Ops:
  1.9 5.5 %collective-permute-start = (f32[376,128]{1,0:T(8,128)S(1)}, f32[376,128]{1,0:T(8,128)S(1)}, u32[]{:S(2)}, u32[]{:S(2)}) collective-permute-start(f32[376,128]{1,0:T(8,128)S(1)} %get-tuple-element.18.refs_0_), channel_id=1, source_target_pairs={{0,4},{5,1},{4,8},{9,5},{8,12},{13,9},{12,14},{15,13},{14,10},{11,... | collective-permute-start | bytes 577544 | tf_op jit(solution)/shard_map/ppermute | solution.py:283
  4.0 6.8 %collective-permute-start.4 = (f32[376,128]{1,0:T(8,128)S(1)}, f32[376,128]{1,0:T(8,128)S(1)}, u32[]{:S(2)}, u32[]{:S(2)}) collective-permute-start(f32[376,128]{1,0:T(8,128)S(1)} %get-tuple-element.19.refs_1_), channel_id=1, source_target_pairs={{4,0},{1,5},{8,4},{5,9},{12,8},{9,13},{14,12},{13,15},{10,14},{15,... | collective-permute-start | bytes 577544 | tf_op jit(solution)/shard_map/ppermute | solution.py:283
  4.1 8.3 %collective-permute-start.8 = (f32[376,128]{1,0:T(8,128)S(1)}, f32[376,128]{1,0:T(8,128)S(1)}, u32[]{:S(2)}, u32[]{:S(2)}) collective-permute-start(f32[376,128]{1,0:T(8,128)S(1)} %get-tuple-element.19.refs_1_), channel_id=1, source_target_pairs={{0,4},{5,1},{4,8},{9,5},{8,12},{13,9},{12,14},{15,13},{14,10},{11,... | collective-permute-start | bytes 577544 | tf_op jit(solution)/shard_map/ppermute | solution.py:283
  5.5 9.4 %collective-permute-start.9 = (f32[376,128]{1,0:T(8,128)S(1)}, f32[376,128]{1,0:T(8,128)S(1)}, u32[]{:S(2)}, u32[]{:S(2)}) collective-permute-start(f32[376,128]{1,0:T(8,128)S(1)} %get-tuple-element.18.refs_0_), channel_id=1, source_target_pairs={{4,0},{1,5},{8,4},{5,9},{12,8},{9,13},{14,12},{13,15},{10,14},{15,... | collective-permute-start | bytes 577544 | tf_op jit(solution)/shard_map/ppermute | solution.py:283
  7.4 10.1 %collective-permute-start.1 = (f32[376,128]{1,0:T(8,128)S(1)}, f32[376,128]{1,0:T(8,128)S(1)}, u32[]{:S(2)}, u32[]{:S(2)}) collective-permute-start(f32[376,128]{1,0:T(8,128)S(1)} %collective-permute-done.refs_0_), channel_id=1, source_target_pairs={{0,4},{5,1},{4,8},{9,5},{8,12},{13,9},{12,14},{15,13},{14,10},{11,... | collective-permute-start | bytes 577544 | tf_op jit(solution)/shard_map/ppermute | solution.py:283
  10.8 8.1 %collective-permute-start.5 = (f32[376,128]{1,0:T(8,128)S(1)}, f32[376,128]{1,0:T(8,128)S(1)}, u32[]{:S(2)}, u32[]{:S(2)}) collective-permute-start(f32[376,128]{1,0:T(8,128)S(1)} %collective-permute-done.4.refs_1_), channel_id=1, source_target_pairs={{4,0},{1,5},{8,4},{5,9},{12,8},{9,13},{14,12},{13,15},{10,14},{15,... | collective-permute-start | bytes 577544 | tf_op jit(solution)/shard_map/ppermute | solution.py:283
  14.9 5.2 %collective-permute-start.10 = (f32[376,128]{1,0:T(8,128)S(1)}, f32[376,128]{1,0:T(8,128)S(1)}, u32[]{:S(2)}, u32[]{:S(2)}) collective-permute-start(f32[376,128]{1,0:T(8,128)S(1)} %collective-permute-done.8.refs_0_), channel_id=1, source_target_pairs={{0,4},{5,1},{4,8},{9,5},{8,12},{13,9},{12,14},{15,13},{14,10},{11,... | collective-permute-start | bytes 577544 | tf_op jit(solution)/shard_map/ppermute | solution.py:283
  16.2 6.6 %collective-permute-start.11 = (f32[376,128]{1,0:T(8,128)S(1)}, f32[376,128]{1,0:T(8,128)S(1)}, u32[]{:S(2)}, u32[]{:S(2)}) collective-permute-start(f32[376,128]{1,0:T(8,128)S(1)} %collective-permute-done.9.refs_1_), channel_id=1, source_target_pairs={{4,0},{1,5},{8,4},{5,9},{12,8},{9,13},{14,12},{13,15},{10,14},{15,... | collective-permute-start | bytes 577544 | tf_op jit(solution)/shard_map/ppermute | solution.py:283
  17.4 8.9 %collective-permute-start.2 = (f32[376,128]{1,0:T(8,128)S(1)}, f32[376,128]{1,0:T(8,128)S(1)}, u32[]{:S(2)}, u32[]{:S(2)}) collective-permute-start(f32[376,128]{1,0:T(8,128)S(1)} %collective-permute-done.1.refs_0_), channel_id=1, source_target_pairs={{0,4},{5,1},{4,8},{9,5},{8,12},{13,9},{12,14},{15,13},{14,10},{11,... | collective-permute-start | bytes 577544 | tf_op jit(solution)/shard_map/ppermute | solution.py:283
  18.9 8.1 %collective-permute-start.6 = (f32[376,128]{1,0:T(8,128)S(1)}, f32[376,128]{1,0:T(8,128)S(1)}, u32[]{:S(2)}, u32[]{:S(2)}) collective-permute-start(f32[376,128]{1,0:T(8,128)S(1)} %collective-permute-done.5.refs_1_), channel_id=1, source_target_pairs={{4,0},{1,5},{8,4},{5,9},{12,8},{9,13},{14,12},{13,15},{10,14},{15,... | collective-permute-start | bytes 577544 | tf_op jit(solution)/shard_map/ppermute | solution.py:283
  22.8 6.1 %collective-permute-start.12 = (f32[376,128]{1,0:T(8,128)S(1)}, f32[376,128]{1,0:T(8,128)S(1)}, u32[]{:S(2)}, u32[]{:S(2)}) collective-permute-start(f32[376,128]{1,0:T(8,128)S(1)} %collective-permute-done.10.refs_0_), channel_id=1, source_target_pairs={{0,4},{5,1},{4,8},{9,5},{8,12},{13,9},{12,14},{15,13},{14,10},{11,... | collective-permute-start | bytes 577544 | tf_op jit(solution)/shard_map/ppermute | solution.py:283
  24.5 6.2 %collective-permute-start.13 = (f32[376,128]{1,0:T(8,128)S(1)}, f32[376,128]{1,0:T(8,128)S(1)}, u32[]{:S(2)}, u32[]{:S(2)}) collective-permute-start(f32[376,128]{1,0:T(8,128)S(1)} %collective-permute-done.11.refs_1_), channel_id=1, source_target_pairs={{4,0},{1,5},{8,4},{5,9},{12,8},{9,13},{14,12},{13,15},{10,14},{15,... | collective-permute-start | bytes 577544 | tf_op jit(solution)/shard_map/ppermute | solution.py:283
  26.3 6.0 %collective-permute-start.3 = (f32[376,128]{1,0:T(8,128)S(1)}, f32[376,128]{1,0:T(8,128)S(1)}, u32[]{:S(2)}, u32[]{:S(2)}) collective-permute-start(f32[376,128]{1,0:T(8,128)S(1)} %collective-permute-done.2.refs_0_), channel_id=1, source_target_pairs={{0,4},{5,1},{4,8},{9,5},{8,12},{13,9},{12,14},{15,13},{14,10},{11,... | collective-permute-start | bytes 577544 | tf_op jit(solution)/shard_map/ppermute | solution.py:283
  27.0 7.9 %collective-permute-start.7 = (f32[376,128]{1,0:T(8,128)S(1)}, f32[376,128]{1,0:T(8,128)S(1)}, u32[]{:S(2)}, u32[]{:S(2)}) collective-permute-start(f32[376,128]{1,0:T(8,128)S(1)} %collective-permute-done.6.refs_1_), channel_id=1, source_target_pairs={{4,0},{1,5},{8,4},{5,9},{12,8},{9,13},{14,12},{13,15},{10,14},{15,... | collective-permute-start | bytes 577544 | tf_op jit(solution)/shard_map/ppermute | solution.py:283
  35.1 2.5 %collective-permute-start.14 = (f32[16,128]{1,0:T(8,128)S(1)}, f32[16,128]{1,0:T(8,128)S(1)}, u32[]{:S(2)}, u32[]{:S(2)}) collective-permute-start(f32[16,128]{1,0:T(8,128)S(1)} %get-tuple-element.30.mine_ref), channel_id=1, source_target_pairs={{0,1},{1,0},{2,3},{3,2},{4,5},{5,4},{6,7},{7,6},{8,9},{9,8},{10,11... | collective-permute-start | bytes 24584 | tf_op jit(solution)/shard_map/ppermute | solution.py:339
  36.6 1.0 %copy-start = (bf16[256,1024]{1,0:T(8,128)(2,1)S(1)}, bf16[256,1024]{1,0:T(8,128)(2,1)}, u32[]{:S(2)}) copy-start(bf16[256,1024]{1,0:T(8,128)(2,1)} %constant.17.clone.col_ref) | copy-start | bytes 1572868
where the time goes:
time: 39.8 us; the launch traced here: 39.2 us
  starting transfers between devices  14.1 us (35%)
  Pallas kernels  13.6 us (34%)
  waiting for transfers between devices  9.84 us (25%)
  local copies, waits for them, and re-layouts  0.99 us (2%)
  between operations  0.79 us (2%)
    ppermute x14, starting transfers between devices, both_ways(): return [lax.ppermute(a, ('tm', 'tile'), way) for a, way in zip(pair, ways)]  12.5 us
    pallas_call x10, Pallas kernels, add_blocks(): pl.pallas_call(lambda *refs: grid_kernel(n, first, last, grids, *refs), o...  10.7 us
    ppermute x14, waiting for transfers between devices, both_ways(): return [lax.ppermute(a, ('tm', 'tile'), way) for a, way in zip(pair, ways)]  9.84 us
    pallas_call x1, Pallas kernels, make_image(): pl.pallas_call(image_kernel, out_shape=jax.ShapeDtypeStruct((POLS, 2, NT_...  1.61 us
    ppermute x1, starting transfers between devices, body(): lax.ppermute(mine, 'tile', [(i, n_tile - 1 - i) for i in range(n_tile)])  1.52 us
    pallas_call x1, Pallas kernels, pack(): pl.pallas_call(lambda *refs: pack_kernel(pieces, *refs), out_shape=[jax.S...  1.24 us
    squeeze x1, local copies, waits for them, and re-layouts, body(): lax.dynamic_index_in_dim(jnp.asarray(row_tables), lax.axis_index('tm'), 0...  0.91 us
  transfers between devices with their start and end apart: 15, of which 6 were waited for; matrix products, arithmetic and copies ran while one was open for 2% of the time, Pallas kernels for 27%

commit v1 on v0

--- a/solution.py
+++ b/solution.py
@@ -223,10 +223,9 @@
                         tiles[pc][pr][:, e * P_SIZE : (e + 1) * P_SIZE] * weights[pc][pr] for pr in range(2)
                     ]
                     cells.append(jnp.concatenate(strip, axis=1))
-            high, low = two_parts(jnp.concatenate(cells, axis=0))
-            both = jnp.dot(row_ref[...], high, preferred_element_type=jnp.float32)
-            rest = jnp.dot(row_ref[:half], low, preferred_element_type=jnp.float32)
-            done.append(both[:half] + both[half:] + rest)
+            cells = jnp.concatenate(cells, axis=0).astype(jnp.bfloat16)
+            both = jnp.dot(row_ref[...], cells, preferred_element_type=jnp.float32)
+            done.append(both[:half] + both[half:])
     high, low = two_parts(jnp.concatenate(done, axis=0))
     both = jnp.dot(high, col_ref[...], preferred_element_type=jnp.float32)
     rest = jnp.dot(low, col_ref[:, : 2 * G], preferred_element_type=jnp.float32)
@@ -293,8 +292,7 @@
         following = both_ways(trailing) if step < n_tm // 2 else None
         acc = add_blocks(acc, trailing)
         trailing = following
-    acc = add_blocks(acc, leading[:1], grids=range(1))
-    acc, sums = add_blocks(acc, leading[1:], last=True, grids=range(1))
+    acc, sums = add_blocks(acc, leading, last=True, grids=range(1))
     return add_blocks(acc, leading, grids=range(1, GRIDS)), sums
 
 

time: 39.8 us -> 39.9 us (level)
  starting transfers between devices: 14.1 us -> 15.2 us
  waiting for transfers between devices: 9.84 us -> 9.01 us
    ppermute x14, starting transfers between devices: 12.5 us -> 14 us  [both_ways(): return [lax.ppermute(a, ('tm', 'tile'), way) for a, way in zip(pair, ways)]]
    ppermute x14, waiting for transfers between devices: 9.84 us -> 9.01 us  [both_ways(): return [lax.ppermute(a, ('tm', 'tile'), way) for a, way in zip(pair, ways)]]
    pallas_call x10 -> x9, Pallas kernels: 10.7 us -> 10.9 us  [add_blocks(): pl.pallas_call(lambda *refs: grid_kernel(n, first, last, grids, *refs), o...]
  transfers between devices with their start and end apart: 15 -> 15, of which waited for: 6 -> 6; matrix products, arithmetic and copies ran while one was open for 2% -> 2% of each run, Pallas kernels for 27% -> 25%
where the time goes in v1:
time: 39.9 us; the launch traced here: 39.5 us
  starting transfers between devices  15.2 us (38%)
  Pallas kernels  13.5 us (34%)
  waiting for transfers between devices  9.01 us (23%)
  local copies, waits for them, and re-layouts  0.92 us (2%)
  between operations  0.81 us (2%)
    ppermute x14, starting transfers between devices, both_ways(): return [lax.ppermute(a, ('tm', 'tile'), way) for a, way in zip(pair, ways)]  14 us
    pallas_call x9, Pallas kernels, add_blocks(): pl.pallas_call(lambda *refs: grid_kernel(n, first, last, grids, *refs), o...  10.9 us
    ppermute x14, waiting for transfers between devices, both_ways(): return [lax.ppermute(a, ('tm', 'tile'), way) for a, way in zip(pair, ways)]  9.01 us
    pallas_call x1, Pallas kernels, make_image(): pl.pallas_call(image_kernel, out_shape=jax.ShapeDtypeStruct((POLS, 2, NT_...  1.37 us
    pallas_call x1, Pallas kernels, pack(): pl.pallas_call(lambda *refs: pack_kernel(pieces, *refs), out_shape=[jax.S...  1.24 us
    ppermute x1, starting transfers between devices, body(): lax.ppermute(mine, 'tile', [(i, n_tile - 1 - i) for i in range(n_tile)])  1.22 us
    squeeze x1, local copies, waits for them, and re-layouts, body(): lax.dynamic_index_in_dim(jnp.asarray(row_tables), lax.axis_index('tm'), 0...  0.91 us
  transfers between devices with their start and end apart: 15, of which 6 were waited for; matrix products, arithmetic and copies ran while one was open for 2% of the time, Pallas kernels for 25%

profile of v1, /device:TPU:1, one launch (start us, length us, event | category | flops | bytes accessed | tf_op | source)
XLA Modules:
  0.0 39.5 jit_solution(13374574262333787603)
XLA Ops:
  0.7 1.2 %pack.1 = (f32[376,128]{1,0:T(8,128)S(1)}, f32[376,128]{1,0:T(8,128)S(1)}) custom-call(f32[16,4,256]{2,1,0:T(4,128)} %bitcast.7, f32[16,256]{1,0:T(8,128)} %bitcast.9, f32[16,2,8,256]{3,2,1,0:T(8,128)} %bitcast.6, s32[16,2,256]{2,1,0:T(2,128)} %bitcast.8, s32[1,16]{1,0:T(1,128)} %refs_4_.1, s32[1,1]{1,0:T(1,128)S(6)} %copy.25.refs_5_), custom_call_target="tpu_custom_call" | custom-call | tf_op jit(solution)/shard_map/pack/pallas_call | solution.py:85
  1.9 2.1 %collective-permute-start = (f32[376,128]{1,0:T(8,128)S(1)}, f32[376,128]{1,0:T(8,128)S(1)}, u32[]{:S(2)}, u32[]{:S(2)}) collective-permute-start(f32[376,128]{1,0:T(8,128)S(1)} %get-tuple-element.18.refs_0_), channel_id=1, source_target_pairs={{0,4},{5,1},{4,8},{9,5},{8,12},{13,9},{12,14},{15,13},{14,10},{11,... | collective-permute-start | bytes 577544 | tf_op jit(solution)/shard_map/ppermute | solution.py:282
  4.0 0.2 collective-permute-start.4
  4.1 1.3 %collective-permute-start.8 = (f32[376,128]{1,0:T(8,128)S(1)}, f32[376,128]{1,0:T(8,128)S(1)}, u32[]{:S(2)}, u32[]{:S(2)}) collective-permute-start(f32[376,128]{1,0:T(8,128)S(1)} %get-tuple-element.19.refs_1_), channel_id=1, source_target_pairs={{0,4},{5,1},{4,8},{9,5},{8,12},{13,9},{12,14},{15,13},{14,10},{11,... | collective-permute-start | bytes 577544 | tf_op jit(solution)/shard_map/ppermute | solution.py:282
  5.5 0.2 collective-permute-start.9
  5.6 0.9 %dynamic-slice_bitcast_fusion.row_ref = bf16[128,512]{1,0:T(8,128)(2,1)S(1)} fusion(bf16[8,128,512]{2,1,0:T(8,128)(2,1)} %constant.16.clone, s32[]{:T(128)S(6)} %select_n.4), kind=kLoop, calls=%fused_computation | loop fusion | bytes 262148 | tf_op jit(solution)/shard_map/jit(dynamic_index_in_dim)/squeeze | solution.py:339
  6.5 0.8 %grid.9.refs_2_ = f32[8,128,640]{2,1,0:T(8,128)S(1)} custom-call(f32[376,128]{1,0:T(8,128)S(1)} %get-tuple-element.18.refs_0_, f32[376,128]{1,0:T(8,128)S(1)} %get-tuple-element.19.refs_1_), custom_call_target="tpu_custom_call" | custom-call | flops 671088640 | bytes 96256 | tf_op jit(solution)/shard_map/grid/pallas_call | solution.py:190
  7.4 0.0 collective-permute-done.refs_0_
  7.4 2.7 %collective-permute-start.1 = (f32[376,128]{1,0:T(8,128)S(1)}, f32[376,128]{1,0:T(8,128)S(1)}, u32[]{:S(2)}, u32[]{:S(2)}) collective-permute-start(f32[376,128]{1,0:T(8,128)S(1)} %collective-permute-done.refs_0_), channel_id=1, source_target_pairs={{0,4},{5,1},{4,8},{9,5},{8,12},{13,9},{12,14},{15,13},{14,10},{11,... | collective-permute-start | bytes 577544 | tf_op jit(solution)/shard_map/ppermute | solution.py:282
  10.1 0.6 %collective-permute-done.4.refs_1_ = f32[376,128]{1,0:T(8,128)S(1)} collective-permute-done((f32[376,128]{1,0:T(8,128)S(1)}, f32[376,128]{1,0:T(8,128)S(1)}, u32[]{:S(2)}, u32[]{:S(2)}) %collective-permute-start.4) | collective-permute-done | bytes 192544 | tf_op jit(solution)/shard_map/ppermute | solution.py:282
  10.8 0.0 collective-permute-start.5
  10.8 2.0 %grid.10.refs_2_ = f32[8,128,640]{2,1,0:T(8,128)S(1)} custom-call(f32[376,128]{1,0:T(8,128)S(1)} %collective-permute-done.refs_0_, f32[376,128]{1,0:T(8,128)S(1)} %collective-permute-done.4.refs_1_, f32[8,128,640]{2,1,0:T(8,128)S(1)} %grid.9.refs_2_), custom_call_target="tpu_custom_call", output_to_operand_aliasing={{}: (2, {})} | custom-call | flops 1342177280 | bytes 96256 | tf_op jit(solution)/shard_map/grid/pallas_call | solution.py:190
  12.8 0.0 collective-permute-done.8.refs_0_
  12.8 2.1 %collective-permute-done.9.refs_1_ = f32[376,128]{1,0:T(8,128)S(1)} collective-permute-done((f32[376,128]{1,0:T(8,128)S(1)}, f32[376,128]{1,0:T(8,128)S(1)}, u32[]{:S(2)}, u32[]{:S(2)}) %collective-permute-start.9) | collective-permute-done | bytes 192544 | tf_op jit(solution)/shard_map/ppermute | solution.py:282
  14.9 1.4 %collective-permute-start.10 = (f32[376,128]{1,0:T(8,128)S(1)}, f32[376,128]{1,0:T(8,128)S(1)}, u32[]{:S(2)}, u32[]{:S(2)}) collective-permute-start(f32[376,128]{1,0:T(8,128)S(1)} %collective-permute-done.8.refs_0_), channel_id=1, source_target_pairs={{0,4},{5,1},{4,8},{9,5},{8,12},{13,9},{12,14},{15,13},{14,10},{11,... | collective-permute-start | bytes 577544 | tf_op jit(solution)/shard_map/ppermute | solution.py:282
  16.2 0.1 collective-permute-start.11
  16.4 2.0 %grid.11.refs_2_ = f32[8,128,640]{2,1,0:T(8,128)S(1)} custom-call(f32[376,128]{1,0:T(8,128)S(1)} %collective-permute-done.8.refs_0_, f32[376,128]{1,0:T(8,128)S(1)} %collective-permute-done.9.refs_1_, f32[8,128,640]{2,1,0:T(8,128)S(1)} %grid.10.refs_2_), custom_call_target="tpu_custom_call", output_to_operand_aliasing={{}: (2, {})} | custom-call | flops 1342177280 | bytes 96256 | tf_op jit(solution)/shard_map/grid/pallas_call | solution.py:190
  18.4 0.0 collective-permute-done.1.refs_0_
  18.4 0.1 collective-permute-start.2
  18.5 0.0 collective-permute-done.5.refs_1_
  18.5 1.4 %collective-permute-start.6 = (f32[376,128]{1,0:T(8,128)S(1)}, f32[376,128]{1,0:T(8,128)S(1)}, u32[]{:S(2)}, u32[]{:S(2)}) collective-permute-start(f32[376,128]{1,0:T(8,128)S(1)} %collective-permute-done.5.refs_1_), channel_id=1, source_target_pairs={{4,0},{1,5},{8,4},{5,9},{12,8},{9,13},{14,12},{13,15},{10,14},{15,... | collective-permute-start | bytes 577544 | tf_op jit(solution)/shard_map/ppermute | solution.py:282
  19.9 0.7 %grid.12.refs_2_ = f32[8,128,640]{2,1,0:T(8,128)S(1)} custom-call(f32[376,128]{1,0:T(8,128)S(1)} %collective-permute-done.1.refs_0_, f32[376,128]{1,0:T(8,128)S(1)} %collective-permute-done.5.refs_1_, f32[8,128,640]{2,1,0:T(8,128)S(1)} %grid.11.refs_2_), custom_call_target="tpu_custom_call", output_to_operand_aliasing={{}: (2, {})} | custom-call | flops 1342177280 | bytes 96256 | tf_op jit(solution)/shard_map/grid/pallas_call | solution.py:190
  20.6 0.0 collective-permute-done.10.refs_0_
  20.6 2.2 %collective-permute-done.11.refs_1_ = f32[376,128]{1,0:T(8,128)S(1)} collective-permute-done((f32[376,128]{1,0:T(8,128)S(1)}, f32[376,128]{1,0:T(8,128)S(1)}, u32[]{:S(2)}, u32[]{:S(2)}) %collective-permute-start.11) | collective-permute-done | bytes 192544 | tf_op jit(solution)/shard_map/ppermute | solution.py:282
  22.8 1.7 %collective-permute-start.12 = (f32[376,128]{1,0:T(8,128)S(1)}, f32[376,128]{1,0:T(8,128)S(1)}, u32[]{:S(2)}, u32[]{:S(2)}) collective-permute-start(f32[376,128]{1,0:T(8,128)S(1)} %collective-permute-done.10.refs_0_), channel_id=1, source_target_pairs={{0,4},{5,1},{4,8},{9,5},{8,12},{13,9},{12,14},{15,13},{14,10},{11,... | collective-permute-start | bytes 577544 | tf_op jit(solution)/shard_map/ppermute | solution.py:282
  24.5 0.0 collective-permute-start.13
  24.5 0.8 %grid.13.refs_2_ = f32[8,128,640]{2,1,0:T(8,128)S(1)} custom-call(f32[376,128]{1,0:T(8,128)S(1)} %collective-permute-done.10.refs_0_, f32[376,128]{1,0:T(8,128)S(1)} %collective-permute-done.11.refs_1_, f32[8,128,640]{2,1,0:T(8,128)S(1)} %grid.12.refs_2_), custom_call_target="tpu_custom_call", output_to_operand_aliasing={{}: (2, {})} | custom-call | flops 1342177280 | bytes 96256 | tf_op jit(solution)/shard_map/grid/pallas_call | solution.py:190
  25.3 0.0 collective-permute-done.2.refs_0_
  25.3 2.9 %collective-permute-start.3 = (f32[376,128]{1,0:T(8,128)S(1)}, f32[376,128]{1,0:T(8,128)S(1)}, u32[]{:S(2)}, u32[]{:S(2)}) collective-permute-start(f32[376,128]{1,0:T(8,128)S(1)} %collective-permute-done.2.refs_0_), channel_id=1, source_target_pairs={{0,4},{5,1},{4,8},{9,5},{8,12},{13,9},{12,14},{15,13},{14,10},{11,... | collective-permute-start | bytes 577544 | tf_op jit(solution)/shard_map/ppermute | solution.py:282
  28.3 0.0 collective-permute-done.6.refs_1_
  28.3 0.0 collective-permute-start.7
  28.3 1.1 %grid.14.refs_2_ = f32[8,128,640]{2,1,0:T(8,128)S(1)} custom-call(f32[376,128]{1,0:T(8,128)S(1)} %collective-permute-done.2.refs_0_, f32[376,128]{1,0:T(8,128)S(1)} %collective-permute-done.6.refs_1_, f32[8,128,640]{2,1,0:T(8,128)S(1)} %grid.13.refs_2_), custom_call_target="tpu_custom_call", output_to_operand_aliasing={{}: (2, {})} | custom-call | flops 1342177280 | bytes 96256 | tf_op jit(solution)/shard_map/grid/pallas_call | solution.py:190
  29.4 0.0 collective-permute-done.12.refs_0_
  29.4 0.8 %collective-permute-done.13.refs_1_ = f32[376,128]{1,0:T(8,128)S(1)} collective-permute-done((f32[376,128]{1,0:T(8,128)S(1)}, f32[376,128]{1,0:T(8,128)S(1)}, u32[]{:S(2)}, u32[]{:S(2)}) %collective-permute-start.13) | collective-permute-done | bytes 192544 | tf_op jit(solution)/shard_map/ppermute | solution.py:282
  30.2 1.1 %grid.15.refs_2_ = f32[8,128,640]{2,1,0:T(8,128)S(1)} custom-call(f32[376,128]{1,0:T(8,128)S(1)} %collective-permute-done.12.refs_0_, f32[376,128]{1,0:T(8,128)S(1)} %collective-permute-done.13.refs_1_, f32[8,128,640]{2,1,0:T(8,128)S(1)} %grid.14.refs_2_), custom_call_target="tpu_custom_call", output_to_operand_aliasing={{}: (2, {})} | custom-call | flops 1342177280 | bytes 96256 | tf_op jit(solution)/shard_map/grid/pallas_call | solution.py:190
  31.2 1.5 %collective-permute-done.3.refs_0_ = f32[376,128]{1,0:T(8,128)S(1)} collective-permute-done((f32[376,128]{1,0:T(8,128)S(1)}, f32[376,128]{1,0:T(8,128)S(1)}, u32[]{:S(2)}, u32[]{:S(2)}) %collective-permute-start.3) | collective-permute-done | bytes 192544 | tf_op jit(solution)/shard_map/ppermute | solution.py:282
  32.7 1.8 %collective-permute-done.7.refs_1_ = f32[376,128]{1,0:T(8,128)S(1)} collective-permute-done((f32[376,128]{1,0:T(8,128)S(1)}, f32[376,128]{1,0:T(8,128)S(1)}, u32[]{:S(2)}, u32[]{:S(2)}) %collective-permute-start.7) | collective-permute-done | bytes 192544 | tf_op jit(solution)/shard_map/ppermute | solution.py:282
  34.5 0.9 %grid.16 = (f32[8,128,640]{2,1,0:T(8,128)S(1)}, f32[16,128]{1,0:T(8,128)S(1)}) custom-call(f32[376,128]{1,0:T(8,128)S(1)} %collective-permute-done.3.refs_0_, f32[376,128]{1,0:T(8,128)S(1)} %collective-permute-done.7.refs_1_, f32[8,128,640]{2,1,0:T(8,128)S(1)} %grid.15.refs_2_), custom_call_target="tpu_custom_call", output_to_operand_aliasing={{0}: (2, {})} | custom-call | flops 268435456 | bytes 96256 | tf_op jit(solution)/shard_map/grid/pallas_call | solution.py:190
  35.4 1.2 %collective-permute-start.14 = (f32[16,128]{1,0:T(8,128)S(1)}, f32[16,128]{1,0:T(8,128)S(1)}, u32[]{:S(2)}, u32[]{:S(2)}) collective-permute-start(f32[16,128]{1,0:T(8,128)S(1)} %get-tuple-element.30.mine_ref), channel_id=1, source_target_pairs={{0,1},{1,0},{2,3},{3,2},{4,5},{5,4},{6,7},{7,6},{8,9},{9,8},{10,11... | collective-permute-start | bytes 24584 | tf_op jit(solution)/shard_map/ppermute | solution.py:337
  36.6 0.0 copy-start
  36.6 1.4 %grid.17.acc_ref = f32[8,128,640]{2,1,0:T(8,128)S(1)} custom-call(f32[376,128]{1,0:T(8,128)S(1)} %collective-permute-done.3.refs_0_, f32[376,128]{1,0:T(8,128)S(1)} %collective-permute-done.7.refs_1_, f32[8,128,640]{2,1,0:T(8,128)S(1)} %get-tuple-element.29.refs_2_), custom_call_target="tpu_custom_call", output_to_operand_aliasing={{}: (2, {})} | custom-call | flops 1073741824 | bytes 96256 | tf_op jit(solution)/shard_map/grid/pallas_call | solution.py:190
  38.1 0.0 collective-permute-done.14.other_ref
  38.1 0.0 copy-done
  38.1 1.4 %image.1 = f32[2,2,2,32,256]{4,3,2,1,0:T(8,128)} custom-call(f32[8,128,640]{2,1,0:T(8,128)S(1)} %grid.17.acc_ref, f32[16,128]{1,0:T(8,128)S(1)} %get-tuple-element.30.mine_ref, f32[16,128]{1,0:T(8,128)S(1)} %collective-permute-done.14.other_ref, bf16[128,512]{1,0:T(8,128)(2,1)S(1)} %dynamic-slice_bitcast_fusion.row_ref, bf16[256,1024]{1,0:T(8,128)(2,1)S(1)} %copy-done), custom_call_target="tpu_custom_call" | custom-call | tf_op jit(solution)/shard_map/image/pallas_call | solution.py:242
Async XLA Ops:
  1.9 5.5 %collective-permute-start = (f32[376,128]{1,0:T(8,128)S(1)}, f32[376,128]{1,0:T(8,128)S(1)}, u32[]{:S(2)}, u32[]{:S(2)}) collective-permute-start(f32[376,128]{1,0:T(8,128)S(1)} %get-tuple-element.18.refs_0_), channel_id=1, source_target_pairs={{0,4},{5,1},{4,8},{9,5},{8,12},{13,9},{12,14},{15,13},{14,10},{11,... | collective-permute-start | bytes 577544 | tf_op jit(solution)/shard_map/ppermute | solution.py:282
  4.0 6.8 %collective-permute-start.4 = (f32[376,128]{1,0:T(8,128)S(1)}, f32[376,128]{1,0:T(8,128)S(1)}, u32[]{:S(2)}, u32[]{:S(2)}) collective-permute-start(f32[376,128]{1,0:T(8,128)S(1)} %get-tuple-element.19.refs_1_), channel_id=1, source_target_pairs={{4,0},{1,5},{8,4},{5,9},{12,8},{9,13},{14,12},{13,15},{10,14},{15,... | collective-permute-start | bytes 577544 | tf_op jit(solution)/shard_map/ppermute | solution.py:282
  4.1 8.7 %collective-permute-start.8 = (f32[376,128]{1,0:T(8,128)S(1)}, f32[376,128]{1,0:T(8,128)S(1)}, u32[]{:S(2)}, u32[]{:S(2)}) collective-permute-start(f32[376,128]{1,0:T(8,128)S(1)} %get-tuple-element.19.refs_1_), channel_id=1, source_target_pairs={{0,4},{5,1},{4,8},{9,5},{8,12},{13,9},{12,14},{15,13},{14,10},{11,... | collective-permute-start | bytes 577544 | tf_op jit(solution)/shard_map/ppermute | solution.py:282
  5.5 9.4 %collective-permute-start.9 = (f32[376,128]{1,0:T(8,128)S(1)}, f32[376,128]{1,0:T(8,128)S(1)}, u32[]{:S(2)}, u32[]{:S(2)}) collective-permute-start(f32[376,128]{1,0:T(8,128)S(1)} %get-tuple-element.18.refs_0_), channel_id=1, source_target_pairs={{4,0},{1,5},{8,4},{5,9},{12,8},{9,13},{14,12},{13,15},{10,14},{15,... | collective-permute-start | bytes 577544 | tf_op jit(solution)/shard_map/ppermute | solution.py:282
  7.4 11.0 %collective-permute-start.1 = (f32[376,128]{1,0:T(8,128)S(1)}, f32[376,128]{1,0:T(8,128)S(1)}, u32[]{:S(2)}, u32[]{:S(2)}) collective-permute-start(f32[376,128]{1,0:T(8,128)S(1)} %collective-permute-done.refs_0_), channel_id=1, source_target_pairs={{0,4},{5,1},{4,8},{9,5},{8,12},{13,9},{12,14},{15,13},{14,10},{11,... | collective-permute-start | bytes 577544 | tf_op jit(solution)/shard_map/ppermute | solution.py:282
  10.8 7.7 %collective-permute-start.5 = (f32[376,128]{1,0:T(8,128)S(1)}, f32[376,128]{1,0:T(8,128)S(1)}, u32[]{:S(2)}, u32[]{:S(2)}) collective-permute-start(f32[376,128]{1,0:T(8,128)S(1)} %collective-permute-done.4.refs_1_), channel_id=1, source_target_pairs={{4,0},{1,5},{8,4},{5,9},{12,8},{9,13},{14,12},{13,15},{10,14},{15,... | collective-permute-start | bytes 577544 | tf_op jit(solution)/shard_map/ppermute | solution.py:282
  14.9 5.7 %collective-permute-start.10 = (f32[376,128]{1,0:T(8,128)S(1)}, f32[376,128]{1,0:T(8,128)S(1)}, u32[]{:S(2)}, u32[]{:S(2)}) collective-permute-start(f32[376,128]{1,0:T(8,128)S(1)} %collective-permute-done.8.refs_0_), channel_id=1, source_target_pairs={{0,4},{5,1},{4,8},{9,5},{8,12},{13,9},{12,14},{15,13},{14,10},{11,... | collective-permute-start | bytes 577544 | tf_op jit(solution)/shard_map/ppermute | solution.py:282
  16.2 6.6 %collective-permute-start.11 = (f32[376,128]{1,0:T(8,128)S(1)}, f32[376,128]{1,0:T(8,128)S(1)}, u32[]{:S(2)}, u32[]{:S(2)}) collective-permute-start(f32[376,128]{1,0:T(8,128)S(1)} %collective-permute-done.9.refs_1_), channel_id=1, source_target_pairs={{4,0},{1,5},{8,4},{5,9},{12,8},{9,13},{14,12},{13,15},{10,14},{15,... | collective-permute-start | bytes 577544 | tf_op jit(solution)/shard_map/ppermute | solution.py:282
  18.4 6.9 %collective-permute-start.2 = (f32[376,128]{1,0:T(8,128)S(1)}, f32[376,128]{1,0:T(8,128)S(1)}, u32[]{:S(2)}, u32[]{:S(2)}) collective-permute-start(f32[376,128]{1,0:T(8,128)S(1)} %collective-permute-done.1.refs_0_), channel_id=1, source_target_pairs={{0,4},{5,1},{4,8},{9,5},{8,12},{13,9},{12,14},{15,13},{14,10},{11,... | collective-permute-start | bytes 577544 | tf_op jit(solution)/shard_map/ppermute | solution.py:282
  18.5 9.8 %collective-permute-start.6 = (f32[376,128]{1,0:T(8,128)S(1)}, f32[376,128]{1,0:T(8,128)S(1)}, u32[]{:S(2)}, u32[]{:S(2)}) collective-permute-start(f32[376,128]{1,0:T(8,128)S(1)} %collective-permute-done.5.refs_1_), channel_id=1, source_target_pairs={{4,0},{1,5},{8,4},{5,9},{12,8},{9,13},{14,12},{13,15},{10,14},{15,... | collective-permute-start | bytes 577544 | tf_op jit(solution)/shard_map/ppermute | solution.py:282
  22.8 6.5 %collective-permute-start.12 = (f32[376,128]{1,0:T(8,128)S(1)}, f32[376,128]{1,0:T(8,128)S(1)}, u32[]{:S(2)}, u32[]{:S(2)}) collective-permute-start(f32[376,128]{1,0:T(8,128)S(1)} %collective-permute-done.10.refs_0_), channel_id=1, source_target_pairs={{0,4},{5,1},{4,8},{9,5},{8,12},{13,9},{12,14},{15,13},{14,10},{11,... | collective-permute-start | bytes 577544 | tf_op jit(solution)/shard_map/ppermute | solution.py:282
  24.5 5.7 %collective-permute-start.13 = (f32[376,128]{1,0:T(8,128)S(1)}, f32[376,128]{1,0:T(8,128)S(1)}, u32[]{:S(2)}, u32[]{:S(2)}) collective-permute-start(f32[376,128]{1,0:T(8,128)S(1)} %collective-permute-done.11.refs_1_), channel_id=1, source_target_pairs={{4,0},{1,5},{8,4},{5,9},{12,8},{9,13},{14,12},{13,15},{10,14},{15,... | collective-permute-start | bytes 577544 | tf_op jit(solution)/shard_map/ppermute | solution.py:282
  25.3 7.4 %collective-permute-start.3 = (f32[376,128]{1,0:T(8,128)S(1)}, f32[376,128]{1,0:T(8,128)S(1)}, u32[]{:S(2)}, u32[]{:S(2)}) collective-permute-start(f32[376,128]{1,0:T(8,128)S(1)} %collective-permute-done.2.refs_0_), channel_id=1, source_target_pairs={{0,4},{5,1},{4,8},{9,5},{8,12},{13,9},{12,14},{15,13},{14,10},{11,... | collective-permute-start | bytes 577544 | tf_op jit(solution)/shard_map/ppermute | solution.py:282
  28.3 6.2 %collective-permute-start.7 = (f32[376,128]{1,0:T(8,128)S(1)}, f32[376,128]{1,0:T(8,128)S(1)}, u32[]{:S(2)}, u32[]{:S(2)}) collective-permute-start(f32[376,128]{1,0:T(8,128)S(1)} %collective-permute-done.6.refs_1_), channel_id=1, source_target_pairs={{4,0},{1,5},{8,4},{5,9},{12,8},{9,13},{14,12},{13,15},{10,14},{15,... | collective-permute-start | bytes 577544 | tf_op jit(solution)/shard_map/ppermute | solution.py:282
  35.4 2.7 %collective-permute-start.14 = (f32[16,128]{1,0:T(8,128)S(1)}, f32[16,128]{1,0:T(8,128)S(1)}, u32[]{:S(2)}, u32[]{:S(2)}) collective-permute-start(f32[16,128]{1,0:T(8,128)S(1)} %get-tuple-element.30.mine_ref), channel_id=1, source_target_pairs={{0,1},{1,0},{2,3},{3,2},{4,5},{5,4},{6,7},{7,6},{8,9},{9,8},{10,11... | collective-permute-start | bytes 24584 | tf_op jit(solution)/shard_map/ppermute | solution.py:337
  36.6 1.5 %copy-start = (bf16[256,1024]{1,0:T(8,128)(2,1)S(1)}, bf16[256,1024]{1,0:T(8,128)(2,1)}, u32[]{:S(2)}) copy-start(bf16[256,1024]{1,0:T(8,128)(2,1)} %constant.17.clone.col_ref) | copy-start | bytes 1572868

commit v2 on v0

--- a/solution.py
+++ b/solution.py
@@ -293,8 +293,7 @@
         following = both_ways(trailing) if step < n_tm // 2 else None
         acc = add_blocks(acc, trailing)
         trailing = following
-    acc = add_blocks(acc, leading[:1], grids=range(1))
-    acc, sums = add_blocks(acc, leading[1:], last=True, grids=range(1))
+    acc, sums = add_blocks(acc, leading, last=True, grids=range(1))
     return add_blocks(acc, leading, grids=range(1, GRIDS)), sums
 
 

time: 39.8 us -> 40.9 us (1.028); the launches traced: 39.2 us -> 40.8 us
  starting transfers between devices: 14.1 us -> 15.1 us
    ppermute x1, starting transfers between devices: 1.52 us -> 2.1 us  [body(): lax.ppermute(mine, 'tile', [(i, n_tile - 1 - i) for i in range(n_tile)])]
    ppermute x14, starting transfers between devices: 12.5 us -> 13 us  [both_ways(): return [lax.ppermute(a, ('tm', 'tile'), way) for a, way in zip(pair, ways)]]
    pallas_call x10 -> x9, Pallas kernels: 10.7 us -> 11 us  [add_blocks(): pl.pallas_call(lambda *refs: grid_kernel(n, first, last, grids, *refs), o...]
  transfers between devices with their start and end apart: 15 -> 15, of which waited for: 6 -> 6; matrix products, arithmetic and copies ran while one was open for 2% -> 2% of each run, Pallas kernels for 27% -> 25%
where the time goes in v2:
time: 40.9 us; the launch traced here: 40.8 us
  starting transfers between devices  15.1 us (37%)
  Pallas kernels  13.9 us (34%)
  waiting for transfers between devices  10.1 us (25%)
  local copies, waits for them, and re-layouts  0.92 us (2%)
  between operations  0.8 us (2%)
    ppermute x14, starting transfers between devices, both_ways(): return [lax.ppermute(a, ('tm', 'tile'), way) for a, way in zip(pair, ways)]  13 us
    pallas_call x9, Pallas kernels, add_blocks(): pl.pallas_call(lambda *refs: grid_kernel(n, first, last, grids, *refs), o...  11 us
    ppermute x14, waiting for transfers between devices, both_ways(): return [lax.ppermute(a, ('tm', 'tile'), way) for a, way in zip(pair, ways)]  10.1 us
    ppermute x1, starting transfers between devices, body(): lax.ppermute(mine, 'tile', [(i, n_tile - 1 - i) for i in range(n_tile)])  2.1 us
    pallas_call x1, Pallas kernels, make_image(): pl.pallas_call(image_kernel, out_shape=jax.ShapeDtypeStruct((POLS, 2, NT_...  1.61 us
    pallas_call x1, Pallas kernels, pack(): pl.pallas_call(lambda *refs: pack_kernel(pieces, *refs), out_shape=[jax.S...  1.24 us
    squeeze x1, local copies, waits for them, and re-layouts, body(): lax.dynamic_index_in_dim(jnp.asarray(row_tables), lax.axis_index('tm'), 0...  0.91 us
  transfers between devices with their start and end apart: 15, of which 6 were waited for; matrix products, arithmetic and copies ran while one was open for 2% of the time, Pallas kernels for 25%

profile of v2, /device:TPU:1, one launch (start us, length us, event | category | flops | bytes accessed | tf_op | source)
XLA Modules:
  0.0 40.8 jit_solution(6902311781225496580)
XLA Ops:
  0.7 1.2 %pack.1 = (f32[376,128]{1,0:T(8,128)S(1)}, f32[376,128]{1,0:T(8,128)S(1)}) custom-call(f32[16,4,256]{2,1,0:T(4,128)} %bitcast.7, f32[16,256]{1,0:T(8,128)} %bitcast.9, f32[16,2,8,256]{3,2,1,0:T(8,128)} %bitcast.6, s32[16,2,256]{2,1,0:T(2,128)} %bitcast.8, s32[1,16]{1,0:T(1,128)} %refs_4_.1, s32[1,1]{1,0:T(1,128)S(6)} %copy.25.refs_5_), custom_call_target="tpu_custom_call" | custom-call | tf_op jit(solution)/shard_map/pack/pallas_call | solution.py:85
  1.9 2.1 %collective-permute-start = (f32[376,128]{1,0:T(8,128)S(1)}, f32[376,128]{1,0:T(8,128)S(1)}, u32[]{:S(2)}, u32[]{:S(2)}) collective-permute-start(f32[376,128]{1,0:T(8,128)S(1)} %get-tuple-element.18.refs_0_), channel_id=1, source_target_pairs={{0,4},{5,1},{4,8},{9,5},{8,12},{13,9},{12,14},{15,13},{14,10},{11,... | collective-permute-start | bytes 577544 | tf_op jit(solution)/shard_map/ppermute | solution.py:283
  4.0 0.2 collective-permute-start.4
  4.1 1.3 %collective-permute-start.8 = (f32[376,128]{1,0:T(8,128)S(1)}, f32[376,128]{1,0:T(8,128)S(1)}, u32[]{:S(2)}, u32[]{:S(2)}) collective-permute-start(f32[376,128]{1,0:T(8,128)S(1)} %get-tuple-element.19.refs_1_), channel_id=1, source_target_pairs={{0,4},{5,1},{4,8},{9,5},{8,12},{13,9},{12,14},{15,13},{14,10},{11,... | collective-permute-start | bytes 577544 | tf_op jit(solution)/shard_map/ppermute | solution.py:283
  5.5 0.2 collective-permute-start.9
  5.6 0.9 %dynamic-slice_bitcast_fusion.row_ref = bf16[128,512]{1,0:T(8,128)(2,1)S(1)} fusion(bf16[8,128,512]{2,1,0:T(8,128)(2,1)} %constant.16.clone, s32[]{:T(128)S(6)} %select_n.4), kind=kLoop, calls=%fused_computation | loop fusion | bytes 262148 | tf_op jit(solution)/shard_map/jit(dynamic_index_in_dim)/squeeze | solution.py:340
  6.5 0.8 %grid.9.refs_2_ = f32[8,128,640]{2,1,0:T(8,128)S(1)} custom-call(f32[376,128]{1,0:T(8,128)S(1)} %get-tuple-element.18.refs_0_, f32[376,128]{1,0:T(8,128)S(1)} %get-tuple-element.19.refs_1_), custom_call_target="tpu_custom_call" | custom-call | flops 671088640 | bytes 96256 | tf_op jit(solution)/shard_map/grid/pallas_call | solution.py:190
  7.4 0.0 collective-permute-done.refs_0_
  7.4 2.2 %collective-permute-start.1 = (f32[376,128]{1,0:T(8,128)S(1)}, f32[376,128]{1,0:T(8,128)S(1)}, u32[]{:S(2)}, u32[]{:S(2)}) collective-permute-start(f32[376,128]{1,0:T(8,128)S(1)} %collective-permute-done.refs_0_), channel_id=1, source_target_pairs={{0,4},{5,1},{4,8},{9,5},{8,12},{13,9},{12,14},{15,13},{14,10},{11,... | collective-permute-start | bytes 577544 | tf_op jit(solution)/shard_map/ppermute | solution.py:283
  9.6 1.2 %collective-permute-done.4.refs_1_ = f32[376,128]{1,0:T(8,128)S(1)} collective-permute-done((f32[376,128]{1,0:T(8,128)S(1)}, f32[376,128]{1,0:T(8,128)S(1)}, u32[]{:S(2)}, u32[]{:S(2)}) %collective-permute-start.4) | collective-permute-done | bytes 192544 | tf_op jit(solution)/shard_map/ppermute | solution.py:283
  10.8 0.0 collective-permute-start.5
  10.8 1.1 %grid.10.refs_2_ = f32[8,128,640]{2,1,0:T(8,128)S(1)} custom-call(f32[376,128]{1,0:T(8,128)S(1)} %collective-permute-done.refs_0_, f32[376,128]{1,0:T(8,128)S(1)} %collective-permute-done.4.refs_1_, f32[8,128,640]{2,1,0:T(8,128)S(1)} %grid.9.refs_2_), custom_call_target="tpu_custom_call", output_to_operand_aliasing={{}: (2, {})} | custom-call | flops 1342177280 | bytes 96256 | tf_op jit(solution)/shard_map/grid/pallas_call | solution.py:190
  11.9 0.0 collective-permute-done.8.refs_0_
  11.9 3.0 %collective-permute-done.9.refs_1_ = f32[376,128]{1,0:T(8,128)S(1)} collective-permute-done((f32[376,128]{1,0:T(8,128)S(1)}, f32[376,128]{1,0:T(8,128)S(1)}, u32[]{:S(2)}, u32[]{:S(2)}) %collective-permute-start.9) | collective-permute-done | bytes 192544 | tf_op jit(solution)/shard_map/ppermute | solution.py:283
  14.9 1.4 %collective-permute-start.10 = (f32[376,128]{1,0:T(8,128)S(1)}, f32[376,128]{1,0:T(8,128)S(1)}, u32[]{:S(2)}, u32[]{:S(2)}) collective-permute-start(f32[376,128]{1,0:T(8,128)S(1)} %collective-permute-done.8.refs_0_), channel_id=1, source_target_pairs={{0,4},{5,1},{4,8},{9,5},{8,12},{13,9},{12,14},{15,13},{14,10},{11,... | collective-permute-start | bytes 577544 | tf_op jit(solution)/shard_map/ppermute | solution.py:283
  16.2 0.1 collective-permute-start.11
  16.4 1.6 %grid.11.refs_2_ = f32[8,128,640]{2,1,0:T(8,128)S(1)} custom-call(f32[376,128]{1,0:T(8,128)S(1)} %collective-permute-done.8.refs_0_, f32[376,128]{1,0:T(8,128)S(1)} %collective-permute-done.9.refs_1_, f32[8,128,640]{2,1,0:T(8,128)S(1)} %grid.10.refs_2_), custom_call_target="tpu_custom_call", output_to_operand_aliasing={{}: (2, {})} | custom-call | flops 1342177280 | bytes 96256 | tf_op jit(solution)/shard_map/grid/pallas_call | solution.py:190
  18.0 0.0 collective-permute-done.1.refs_0_
  18.0 0.4 %collective-permute-start.2 = (f32[376,128]{1,0:T(8,128)S(1)}, f32[376,128]{1,0:T(8,128)S(1)}, u32[]{:S(2)}, u32[]{:S(2)}) collective-permute-start(f32[376,128]{1,0:T(8,128)S(1)} %collective-permute-done.1.refs_0_), channel_id=1, source_target_pairs={{0,4},{5,1},{4,8},{9,5},{8,12},{13,9},{12,14},{15,13},{14,10},{11,... | collective-permute-start | bytes 577544 | tf_op jit(solution)/shard_map/ppermute | solution.py:283
  18.4 0.0 collective-permute-done.5.refs_1_
  18.4 1.1 %collective-permute-start.6 = (f32[376,128]{1,0:T(8,128)S(1)}, f32[376,128]{1,0:T(8,128)S(1)}, u32[]{:S(2)}, u32[]{:S(2)}) collective-permute-start(f32[376,128]{1,0:T(8,128)S(1)} %collective-permute-done.5.refs_1_), channel_id=1, source_target_pairs={{4,0},{1,5},{8,4},{5,9},{12,8},{9,13},{14,12},{13,15},{10,14},{15,... | collective-permute-start | bytes 577544 | tf_op jit(solution)/shard_map/ppermute | solution.py:283
  19.5 0.7 %grid.12.refs_2_ = f32[8,128,640]{2,1,0:T(8,128)S(1)} custom-call(f32[376,128]{1,0:T(8,128)S(1)} %collective-permute-done.1.refs_0_, f32[376,128]{1,0:T(8,128)S(1)} %collective-permute-done.5.refs_1_, f32[8,128,640]{2,1,0:T(8,128)S(1)} %grid.11.refs_2_), custom_call_target="tpu_custom_call", output_to_operand_aliasing={{}: (2, {})} | custom-call | flops 1342177280 | bytes 96256 | tf_op jit(solution)/shard_map/grid/pallas_call | solution.py:190
  20.2 0.0 collective-permute-done.10.refs_0_
  20.2 2.6 %collective-permute-done.11.refs_1_ = f32[376,128]{1,0:T(8,128)S(1)} collective-permute-done((f32[376,128]{1,0:T(8,128)S(1)}, f32[376,128]{1,0:T(8,128)S(1)}, u32[]{:S(2)}, u32[]{:S(2)}) %collective-permute-start.11) | collective-permute-done | bytes 192544 | tf_op jit(solution)/shard_map/ppermute | solution.py:283
  22.8 1.7 %collective-permute-start.12 = (f32[376,128]{1,0:T(8,128)S(1)}, f32[376,128]{1,0:T(8,128)S(1)}, u32[]{:S(2)}, u32[]{:S(2)}) collective-permute-start(f32[376,128]{1,0:T(8,128)S(1)} %collective-permute-done.10.refs_0_), channel_id=1, source_target_pairs={{0,4},{5,1},{4,8},{9,5},{8,12},{13,9},{12,14},{15,13},{14,10},{11,... | collective-permute-start | bytes 577544 | tf_op jit(solution)/shard_map/ppermute | solution.py:283
  24.5 0.0 collective-permute-start.13
  24.5 0.8 %grid.13.refs_2_ = f32[8,128,640]{2,1,0:T(8,128)S(1)} custom-call(f32[376,128]{1,0:T(8,128)S(1)} %collective-permute-done.10.refs_0_, f32[376,128]{1,0:T(8,128)S(1)} %collective-permute-done.11.refs_1_, f32[8,128,640]{2,1,0:T(8,128)S(1)} %grid.12.refs_2_), custom_call_target="tpu_custom_call", output_to_operand_aliasing={{}: (2, {})} | custom-call | flops 1342177280 | bytes 96256 | tf_op jit(solution)/shard_map/grid/pallas_call | solution.py:190
  25.3 0.0 collective-permute-done.2.refs_0_
  25.3 2.5 %collective-permute-start.3 = (f32[376,128]{1,0:T(8,128)S(1)}, f32[376,128]{1,0:T(8,128)S(1)}, u32[]{:S(2)}, u32[]{:S(2)}) collective-permute-start(f32[376,128]{1,0:T(8,128)S(1)} %collective-permute-done.2.refs_0_), channel_id=1, source_target_pairs={{0,4},{5,1},{4,8},{9,5},{8,12},{13,9},{12,14},{15,13},{14,10},{11,... | collective-permute-start | bytes 577544 | tf_op jit(solution)/shard_map/ppermute | solution.py:283
  27.8 0.0 collective-permute-done.6.refs_1_
  27.8 0.0 collective-permute-start.7
  27.9 1.6 %grid.14.refs_2_ = f32[8,128,640]{2,1,0:T(8,128)S(1)} custom-call(f32[376,128]{1,0:T(8,128)S(1)} %collective-permute-done.2.refs_0_, f32[376,128]{1,0:T(8,128)S(1)} %collective-permute-done.6.refs_1_, f32[8,128,640]{2,1,0:T(8,128)S(1)} %grid.13.refs_2_), custom_call_target="tpu_custom_call", output_to_operand_aliasing={{}: (2, {})} | custom-call | flops 1342177280 | bytes 96256 | tf_op jit(solution)/shard_map/grid/pallas_call | solution.py:190
  29.5 0.0 collective-permute-done.12.refs_0_
  29.5 0.5 %collective-permute-done.13.refs_1_ = f32[376,128]{1,0:T(8,128)S(1)} collective-permute-done((f32[376,128]{1,0:T(8,128)S(1)}, f32[376,128]{1,0:T(8,128)S(1)}, u32[]{:S(2)}, u32[]{:S(2)}) %collective-permute-start.13) | collective-permute-done | bytes 192544 | tf_op jit(solution)/shard_map/ppermute | solution.py:283
  30.0 2.1 %grid.15.refs_2_ = f32[8,128,640]{2,1,0:T(8,128)S(1)} custom-call(f32[376,128]{1,0:T(8,128)S(1)} %collective-permute-done.12.refs_0_, f32[376,128]{1,0:T(8,128)S(1)} %collective-permute-done.13.refs_1_, f32[8,128,640]{2,1,0:T(8,128)S(1)} %grid.14.refs_2_), custom_call_target="tpu_custom_call", output_to_operand_aliasing={{}: (2, {})} | custom-call | flops 1342177280 | bytes 96256 | tf_op jit(solution)/shard_map/grid/pallas_call | solution.py:190
  32.1 0.3 collective-permute-done.3.refs_0_
  32.4 2.4 %collective-permute-done.7.refs_1_ = f32[376,128]{1,0:T(8,128)S(1)} collective-permute-done((f32[376,128]{1,0:T(8,128)S(1)}, f32[376,128]{1,0:T(8,128)S(1)}, u32[]{:S(2)}, u32[]{:S(2)}) %collective-permute-start.7) | collective-permute-done | bytes 192544 | tf_op jit(solution)/shard_map/ppermute | solution.py:283
  34.7 0.9 %grid.16 = (f32[8,128,640]{2,1,0:T(8,128)S(1)}, f32[16,128]{1,0:T(8,128)S(1)}) custom-call(f32[376,128]{1,0:T(8,128)S(1)} %collective-permute-done.3.refs_0_, f32[376,128]{1,0:T(8,128)S(1)} %collective-permute-done.7.refs_1_, f32[8,128,640]{2,1,0:T(8,128)S(1)} %grid.15.refs_2_), custom_call_target="tpu_custom_call", output_to_operand_aliasing={{0}: (2, {})} | custom-call | flops 268435456 | bytes 96256 | tf_op jit(solution)/shard_map/grid/pallas_call | solution.py:190
  35.7 2.1 %collective-permute-start.14 = (f32[16,128]{1,0:T(8,128)S(1)}, f32[16,128]{1,0:T(8,128)S(1)}, u32[]{:S(2)}, u32[]{:S(2)}) collective-permute-start(f32[16,128]{1,0:T(8,128)S(1)} %get-tuple-element.30.mine_ref), channel_id=1, source_target_pairs={{0,1},{1,0},{2,3},{3,2},{4,5},{5,4},{6,7},{7,6},{8,9},{9,8},{10,11... | collective-permute-start | bytes 24584 | tf_op jit(solution)/shard_map/ppermute | solution.py:338
  37.8 0.0 copy-start
  37.8 1.4 %grid.17.acc_ref = f32[8,128,640]{2,1,0:T(8,128)S(1)} custom-call(f32[376,128]{1,0:T(8,128)S(1)} %collective-permute-done.3.refs_0_, f32[376,128]{1,0:T(8,128)S(1)} %collective-permute-done.7.refs_1_, f32[8,128,640]{2,1,0:T(8,128)S(1)} %get-tuple-element.29.refs_2_), custom_call_target="tpu_custom_call", output_to_operand_aliasing={{}: (2, {})} | custom-call | flops 1073741824 | bytes 96256 | tf_op jit(solution)/shard_map/grid/pallas_call | solution.py:190
  39.2 0.0 collective-permute-done.14.other_ref
  39.2 0.0 copy-done
  39.2 1.6 %image.1 = f32[2,2,2,32,256]{4,3,2,1,0:T(8,128)} custom-call(f32[8,128,640]{2,1,0:T(8,128)S(1)} %grid.17.acc_ref, f32[16,128]{1,0:T(8,128)S(1)} %get-tuple-element.30.mine_ref, f32[16,128]{1,0:T(8,128)S(1)} %collective-permute-done.14.other_ref, bf16[128,512]{1,0:T(8,128)(2,1)S(1)} %dynamic-slice_bitcast_fusion.row_ref, bf16[256,1024]{1,0:T(8,128)(2,1)S(1)} %copy-done), custom_call_target="tpu_custom_call" | custom-call | tf_op jit(solution)/shard_map/image/pallas_call | solution.py:243
Async XLA Ops:
  1.9 5.5 %collective-permute-start = (f32[376,128]{1,0:T(8,128)S(1)}, f32[376,128]{1,0:T(8,128)S(1)}, u32[]{:S(2)}, u32[]{:S(2)}) collective-permute-start(f32[376,128]{1,0:T(8,128)S(1)} %get-tuple-element.18.refs_0_), channel_id=1, source_target_pairs={{0,4},{5,1},{4,8},{9,5},{8,12},{13,9},{12,14},{15,13},{14,10},{11,... | collective-permute-start | bytes 577544 | tf_op jit(solution)/shard_map/ppermute | solution.py:283
  4.0 6.8 %collective-permute-start.4 = (f32[376,128]{1,0:T(8,128)S(1)}, f32[376,128]{1,0:T(8,128)S(1)}, u32[]{:S(2)}, u32[]{:S(2)}) collective-permute-start(f32[376,128]{1,0:T(8,128)S(1)} %get-tuple-element.19.refs_1_), channel_id=1, source_target_pairs={{4,0},{1,5},{8,4},{5,9},{12,8},{9,13},{14,12},{13,15},{10,14},{15,... | collective-permute-start | bytes 577544 | tf_op jit(solution)/shard_map/ppermute | solution.py:283
  4.1 7.7 %collective-permute-start.8 = (f32[376,128]{1,0:T(8,128)S(1)}, f32[376,128]{1,0:T(8,128)S(1)}, u32[]{:S(2)}, u32[]{:S(2)}) collective-permute-start(f32[376,128]{1,0:T(8,128)S(1)} %get-tuple-element.19.refs_1_), channel_id=1, source_target_pairs={{0,4},{5,1},{4,8},{9,5},{8,12},{13,9},{12,14},{15,13},{14,10},{11,... | collective-permute-start | bytes 577544 | tf_op jit(solution)/shard_map/ppermute | solution.py:283
  5.5 9.4 %collective-permute-start.9 = (f32[376,128]{1,0:T(8,128)S(1)}, f32[376,128]{1,0:T(8,128)S(1)}, u32[]{:S(2)}, u32[]{:S(2)}) collective-permute-start(f32[376,128]{1,0:T(8,128)S(1)} %get-tuple-element.18.refs_0_), channel_id=1, source_target_pairs={{4,0},{1,5},{8,4},{5,9},{12,8},{9,13},{14,12},{13,15},{10,14},{15,... | collective-permute-start | bytes 577544 | tf_op jit(solution)/shard_map/ppermute | solution.py:283
  7.4 10.6 %collective-permute-start.1 = (f32[376,128]{1,0:T(8,128)S(1)}, f32[376,128]{1,0:T(8,128)S(1)}, u32[]{:S(2)}, u32[]{:S(2)}) collective-permute-start(f32[376,128]{1,0:T(8,128)S(1)} %collective-permute-done.refs_0_), channel_id=1, source_target_pairs={{0,4},{5,1},{4,8},{9,5},{8,12},{13,9},{12,14},{15,13},{14,10},{11,... | collective-permute-start | bytes 577544 | tf_op jit(solution)/shard_map/ppermute | solution.py:283
  10.8 7.7 %collective-permute-start.5 = (f32[376,128]{1,0:T(8,128)S(1)}, f32[376,128]{1,0:T(8,128)S(1)}, u32[]{:S(2)}, u32[]{:S(2)}) collective-permute-start(f32[376,128]{1,0:T(8,128)S(1)} %collective-permute-done.4.refs_1_), channel_id=1, source_target_pairs={{4,0},{1,5},{8,4},{5,9},{12,8},{9,13},{14,12},{13,15},{10,14},{15,... | collective-permute-start | bytes 577544 | tf_op jit(solution)/shard_map/ppermute | solution.py:283
  14.9 5.3 %collective-permute-start.10 = (f32[376,128]{1,0:T(8,128)S(1)}, f32[376,128]{1,0:T(8,128)S(1)}, u32[]{:S(2)}, u32[]{:S(2)}) collective-permute-start(f32[376,128]{1,0:T(8,128)S(1)} %collective-permute-done.8.refs_0_), channel_id=1, source_target_pairs={{0,4},{5,1},{4,8},{9,5},{8,12},{13,9},{12,14},{15,13},{14,10},{11,... | collective-permute-start | bytes 577544 | tf_op jit(solution)/shard_map/ppermute | solution.py:283
  16.2 6.6 %collective-permute-start.11 = (f32[376,128]{1,0:T(8,128)S(1)}, f32[376,128]{1,0:T(8,128)S(1)}, u32[]{:S(2)}, u32[]{:S(2)}) collective-permute-start(f32[376,128]{1,0:T(8,128)S(1)} %collective-permute-done.9.refs_1_), channel_id=1, source_target_pairs={{4,0},{1,5},{8,4},{5,9},{12,8},{9,13},{14,12},{13,15},{10,14},{15,... | collective-permute-start | bytes 577544 | tf_op jit(solution)/shard_map/ppermute | solution.py:283
  18.0 7.3 %collective-permute-start.2 = (f32[376,128]{1,0:T(8,128)S(1)}, f32[376,128]{1,0:T(8,128)S(1)}, u32[]{:S(2)}, u32[]{:S(2)}) collective-permute-start(f32[376,128]{1,0:T(8,128)S(1)} %collective-permute-done.1.refs_0_), channel_id=1, source_target_pairs={{0,4},{5,1},{4,8},{9,5},{8,12},{13,9},{12,14},{15,13},{14,10},{11,... | collective-permute-start | bytes 577544 | tf_op jit(solution)/shard_map/ppermute | solution.py:283
  18.4 9.4 %collective-permute-start.6 = (f32[376,128]{1,0:T(8,128)S(1)}, f32[376,128]{1,0:T(8,128)S(1)}, u32[]{:S(2)}, u32[]{:S(2)}) collective-permute-start(f32[376,128]{1,0:T(8,128)S(1)} %collective-permute-done.5.refs_1_), channel_id=1, source_target_pairs={{4,0},{1,5},{8,4},{5,9},{12,8},{9,13},{14,12},{13,15},{10,14},{15,... | collective-permute-start | bytes 577544 | tf_op jit(solution)/shard_map/ppermute | solution.py:283
  22.8 6.7 %collective-permute-start.12 = (f32[376,128]{1,0:T(8,128)S(1)}, f32[376,128]{1,0:T(8,128)S(1)}, u32[]{:S(2)}, u32[]{:S(2)}) collective-permute-start(f32[376,128]{1,0:T(8,128)S(1)} %collective-permute-done.10.refs_0_), channel_id=1, source_target_pairs={{0,4},{5,1},{4,8},{9,5},{8,12},{13,9},{12,14},{15,13},{14,10},{11,... | collective-permute-start | bytes 577544 | tf_op jit(solution)/shard_map/ppermute | solution.py:283
  24.5 5.5 %collective-permute-start.13 = (f32[376,128]{1,0:T(8,128)S(1)}, f32[376,128]{1,0:T(8,128)S(1)}, u32[]{:S(2)}, u32[]{:S(2)}) collective-permute-start(f32[376,128]{1,0:T(8,128)S(1)} %collective-permute-done.11.refs_1_), channel_id=1, source_target_pairs={{4,0},{1,5},{8,4},{5,9},{12,8},{9,13},{14,12},{13,15},{10,14},{15,... | collective-permute-start | bytes 577544 | tf_op jit(solution)/shard_map/ppermute | solution.py:283
  25.3 7.0 %collective-permute-start.3 = (f32[376,128]{1,0:T(8,128)S(1)}, f32[376,128]{1,0:T(8,128)S(1)}, u32[]{:S(2)}, u32[]{:S(2)}) collective-permute-start(f32[376,128]{1,0:T(8,128)S(1)} %collective-permute-done.2.refs_0_), channel_id=1, source_target_pairs={{0,4},{5,1},{4,8},{9,5},{8,12},{13,9},{12,14},{15,13},{14,10},{11,... | collective-permute-start | bytes 577544 | tf_op jit(solution)/shard_map/ppermute | solution.py:283
  27.8 6.9 %collective-permute-start.7 = (f32[376,128]{1,0:T(8,128)S(1)}, f32[376,128]{1,0:T(8,128)S(1)}, u32[]{:S(2)}, u32[]{:S(2)}) collective-permute-start(f32[376,128]{1,0:T(8,128)S(1)} %collective-permute-done.6.refs_1_), channel_id=1, source_target_pairs={{4,0},{1,5},{8,4},{5,9},{12,8},{9,13},{14,12},{13,15},{10,14},{15,... | collective-permute-start | bytes 577544 | tf_op jit(solution)/shard_map/ppermute | solution.py:283
  35.7 3.5 %collective-permute-start.14 = (f32[16,128]{1,0:T(8,128)S(1)}, f32[16,128]{1,0:T(8,128)S(1)}, u32[]{:S(2)}, u32[]{:S(2)}) collective-permute-start(f32[16,128]{1,0:T(8,128)S(1)} %get-tuple-element.30.mine_ref), channel_id=1, source_target_pairs={{0,1},{1,0},{2,3},{3,2},{4,5},{5,4},{6,7},{7,6},{8,9},{9,8},{10,11... | collective-permute-start | bytes 24584 | tf_op jit(solution)/shard_map/ppermute | solution.py:338
  37.8 1.5 %copy-start = (bf16[256,1024]{1,0:T(8,128)(2,1)S(1)}, bf16[256,1024]{1,0:T(8,128)(2,1)}, u32[]{:S(2)}) copy-start(bf16[256,1024]{1,0:T(8,128)(2,1)} %constant.17.clone.col_ref) | copy-start | bytes 1572868

commit v3 on v2

--- a/solution.py
+++ b/solution.py
@@ -284,10 +284,10 @@
 
     leading = both_ways(packed)
     trailing = both_ways(packed[::-1])
-    acc = add_blocks(None, packed)
+    acc = add_blocks(None, packed[:1])
     for step in range(2, n_tm // 2 + 1):
         following = both_ways(leading)
-        acc = add_blocks(acc, leading)
+        acc = add_blocks(acc, leading + (list(packed[1:]) if step == 2 else []))
         acc, *trailing = lax.optimization_barrier((acc, *trailing))
         leading = following
         following = both_ways(trailing) if step < n_tm // 2 else None

time: 40.9 us -> 40.6 us (level)
  no operation moved by 1% of the time
where the time goes in v3:
time: 40.6 us; the launch traced here: 40.3 us
  starting transfers between devices  14.8 us (36%)
  Pallas kernels  13.6 us (33%)
  waiting for transfers between devices  10.1 us (25%)
  local copies, waits for them, and re-layouts  1 us (2%)
  between operations  0.8 us (2%)
    ppermute x14, starting transfers between devices, both_ways(): return [lax.ppermute(a, ('tm', 'tile'), way) for a, way in zip(pair, ways)]  12.7 us
    pallas_call x9, Pallas kernels, add_blocks(): pl.pallas_call(lambda *refs: grid_kernel(n, first, last, grids, *refs), o...  10.7 us
    ppermute x14, waiting for transfers between devices, both_ways(): return [lax.ppermute(a, ('tm', 'tile'), way) for a, way in zip(pair, ways)]  10.1 us
    ppermute x1, starting transfers between devices, body(): lax.ppermute(mine, 'tile', [(i, n_tile - 1 - i) for i in range(n_tile)])  2.12 us
    pallas_call x1, Pallas kernels, make_image(): pl.pallas_call(image_kernel, out_shape=jax.ShapeDtypeStruct((POLS, 2, NT_...  1.64 us
    pallas_call x1, Pallas kernels, pack(): pl.pallas_call(lambda *refs: pack_kernel(pieces, *refs), out_shape=[jax.S...  1.24 us
    squeeze x1, local copies, waits for them, and re-layouts, body(): lax.dynamic_index_in_dim(jnp.asarray(row_tables), lax.axis_index('tm'), 0...  0.91 us
  transfers between devices with their start and end apart: 15, of which 6 were waited for; matrix products, arithmetic and copies ran while one was open for 2% of the time, Pallas kernels for 25%

profile of v3, /device:TPU:1, one launch (start us, length us, event | category | flops | bytes accessed | tf_op | source)
XLA Modules:
  0.0 40.3 jit_solution(12241222502946936478)
XLA Ops:
  0.7 1.2 %pack.1 = (f32[376,128]{1,0:T(8,128)S(1)}, f32[376,128]{1,0:T(8,128)S(1)}) custom-call(f32[16,4,256]{2,1,0:T(4,128)} %bitcast.7, f32[16,256]{1,0:T(8,128)} %bitcast.9, f32[16,2,8,256]{3,2,1,0:T(8,128)} %bitcast.6, s32[16,2,256]{2,1,0:T(2,128)} %bitcast.8, s32[1,16]{1,0:T(1,128)} %refs_4_.1, s32[1,1]{1,0:T(1,128)S(6)} %copy.25.refs_5_), custom_call_target="tpu_custom_call" | custom-call | tf_op jit(solution)/shard_map/pack/pallas_call | solution.py:85
  1.9 2.1 %collective-permute-start = (f32[376,128]{1,0:T(8,128)S(1)}, f32[376,128]{1,0:T(8,128)S(1)}, u32[]{:S(2)}, u32[]{:S(2)}) collective-permute-start(f32[376,128]{1,0:T(8,128)S(1)} %get-tuple-element.18.refs_0_), channel_id=1, source_target_pairs={{0,4},{5,1},{4,8},{9,5},{8,12},{13,9},{12,14},{15,13},{14,10},{11,... | collective-permute-start | bytes 577544 | tf_op jit(solution)/shard_map/ppermute | solution.py:283
  4.0 0.2 collective-permute-start.4
  4.1 1.3 %collective-permute-start.8 = (f32[376,128]{1,0:T(8,128)S(1)}, f32[376,128]{1,0:T(8,128)S(1)}, u32[]{:S(2)}, u32[]{:S(2)}) collective-permute-start(f32[376,128]{1,0:T(8,128)S(1)} %get-tuple-element.19.refs_2_), channel_id=1, source_target_pairs={{0,4},{5,1},{4,8},{9,5},{8,12},{13,9},{12,14},{15,13},{14,10},{11,... | collective-permute-start | bytes 577544 | tf_op jit(solution)/shard_map/ppermute | solution.py:283
  5.5 0.2 collective-permute-start.9
  5.6 0.9 %dynamic-slice_bitcast_fusion.row_ref = bf16[128,512]{1,0:T(8,128)(2,1)S(1)} fusion(bf16[8,128,512]{2,1,0:T(8,128)(2,1)} %constant.16.clone, s32[]{:T(128)S(6)} %select_n.4), kind=kLoop, calls=%fused_computation | loop fusion | bytes 262148 | tf_op jit(solution)/shard_map/jit(dynamic_index_in_dim)/squeeze | solution.py:340
  6.5 1.2 %grid.9.refs_3_ = f32[8,128,640]{2,1,0:T(8,128)S(1)} custom-call(f32[376,128]{1,0:T(8,128)S(1)} %get-tuple-element.18.refs_0_), custom_call_target="tpu_custom_call" | custom-call | flops 335544320 | bytes 48128 | tf_op jit(solution)/shard_map/grid/pallas_call | solution.py:190
  7.7 0.0 collective-permute-done.refs_0_
  7.7 1.8 %collective-permute-start.1 = (f32[376,128]{1,0:T(8,128)S(1)}, f32[376,128]{1,0:T(8,128)S(1)}, u32[]{:S(2)}, u32[]{:S(2)}) collective-permute-start(f32[376,128]{1,0:T(8,128)S(1)} %collective-permute-done.refs_0_), channel_id=1, source_target_pairs={{0,4},{5,1},{4,8},{9,5},{8,12},{13,9},{12,14},{15,13},{14,10},{11,... | collective-permute-start | bytes 577544 | tf_op jit(solution)/shard_map/ppermute | solution.py:283
  9.6 1.2 %collective-permute-done.4.refs_1_ = f32[376,128]{1,0:T(8,128)S(1)} collective-permute-done((f32[376,128]{1,0:T(8,128)S(1)}, f32[376,128]{1,0:T(8,128)S(1)}, u32[]{:S(2)}, u32[]{:S(2)}) %collective-permute-start.4) | collective-permute-done | bytes 192544 | tf_op jit(solution)/shard_map/ppermute | solution.py:283
  10.8 0.0 collective-permute-start.5
  10.8 2.1 %grid.10.refs_2_ = f32[8,128,640]{2,1,0:T(8,128)S(1)} custom-call(f32[376,128]{1,0:T(8,128)S(1)} %collective-permute-done.refs_0_, f32[376,128]{1,0:T(8,128)S(1)} %collective-permute-done.4.refs_1_, f32[376,128]{1,0:T(8,128)S(1)} %get-tuple-element.19.refs_2_, f32[8,128,640]{2,1,0:T(8,128)S(1)} %grid.9.refs_3_), custom_call_target="tpu_custom_call", output_to_operand_aliasing={{}: (3, {})} | custom-call | flops 2013265920 | bytes 144384 | tf_op jit(solution)/shard_map/grid/pallas_call | solution.py:190
  12.9 0.0 collective-permute-done.8.refs_0_
  12.9 2.0 %collective-permute-done.9.refs_1_ = f32[376,128]{1,0:T(8,128)S(1)} collective-permute-done((f32[376,128]{1,0:T(8,128)S(1)}, f32[376,128]{1,0:T(8,128)S(1)}, u32[]{:S(2)}, u32[]{:S(2)}) %collective-permute-start.9) | collective-permute-done | bytes 192544 | tf_op jit(solution)/shard_map/ppermute | solution.py:283
  14.9 1.4 %collective-permute-start.10 = (f32[376,128]{1,0:T(8,128)S(1)}, f32[376,128]{1,0:T(8,128)S(1)}, u32[]{:S(2)}, u32[]{:S(2)}) collective-permute-start(f32[376,128]{1,0:T(8,128)S(1)} %collective-permute-done.8.refs_0_), channel_id=1, source_target_pairs={{0,4},{5,1},{4,8},{9,5},{8,12},{13,9},{12,14},{15,13},{14,10},{11,... | collective-permute-start | bytes 577544 | tf_op jit(solution)/shard_map/ppermute | solution.py:283
  16.2 0.1 collective-permute-start.11
  16.4 1.2 %grid.11.refs_2_ = f32[8,128,640]{2,1,0:T(8,128)S(1)} custom-call(f32[376,128]{1,0:T(8,128)S(1)} %collective-permute-done.8.refs_0_, f32[376,128]{1,0:T(8,128)S(1)} %collective-permute-done.9.refs_1_, f32[8,128,640]{2,1,0:T(8,128)S(1)} %grid.10.refs_2_), custom_call_target="tpu_custom_call", output_to_operand_aliasing={{}: (2, {})} | custom-call | flops 1342177280 | bytes 96256 | tf_op jit(solution)/shard_map/grid/pallas_call | solution.py:190
  17.6 0.0 collective-permute-done.1.refs_0_
  17.6 1.8 %collective-permute-start.2 = (f32[376,128]{1,0:T(8,128)S(1)}, f32[376,128]{1,0:T(8,128)S(1)}, u32[]{:S(2)}, u32[]{:S(2)}) collective-permute-start(f32[376,128]{1,0:T(8,128)S(1)} %collective-permute-done.1.refs_0_), channel_id=1, source_target_pairs={{0,4},{5,1},{4,8},{9,5},{8,12},{13,9},{12,14},{15,13},{14,10},{11,... | collective-permute-start | bytes 577544 | tf_op jit(solution)/shard_map/ppermute | solution.py:283
  19.4 0.0 collective-permute-done.5.refs_1_
  19.4 0.0 collective-permute-start.6
  19.4 0.7 %grid.12.refs_2_ = f32[8,128,640]{2,1,0:T(8,128)S(1)} custom-call(f32[376,128]{1,0:T(8,128)S(1)} %collective-permute-done.1.refs_0_, f32[376,128]{1,0:T(8,128)S(1)} %collective-permute-done.5.refs_1_, f32[8,128,640]{2,1,0:T(8,128)S(1)} %grid.11.refs_2_), custom_call_target="tpu_custom_call", output_to_operand_aliasing={{}: (2, {})} | custom-call | flops 1342177280 | bytes 96256 | tf_op jit(solution)/shard_map/grid/pallas_call | solution.py:190
  20.1 0.0 collective-permute-done.10.refs_0_
  20.1 2.7 %collective-permute-done.11.refs_1_ = f32[376,128]{1,0:T(8,128)S(1)} collective-permute-done((f32[376,128]{1,0:T(8,128)S(1)}, f32[376,128]{1,0:T(8,128)S(1)}, u32[]{:S(2)}, u32[]{:S(2)}) %collective-permute-start.11) | collective-permute-done | bytes 192544 | tf_op jit(solution)/shard_map/ppermute | solution.py:283
  22.8 1.1 %collective-permute-start.12 = (f32[376,128]{1,0:T(8,128)S(1)}, f32[376,128]{1,0:T(8,128)S(1)}, u32[]{:S(2)}, u32[]{:S(2)}) collective-permute-start(f32[376,128]{1,0:T(8,128)S(1)} %collective-permute-done.10.refs_0_), channel_id=1, source_target_pairs={{0,4},{5,1},{4,8},{9,5},{8,12},{13,9},{12,14},{15,13},{14,10},{11,... | collective-permute-start | bytes 577544 | tf_op jit(solution)/shard_map/ppermute | solution.py:283
  23.9 0.4 collective-permute-start.13
  24.3 0.8 %grid.13.refs_2_ = f32[8,128,640]{2,1,0:T(8,128)S(1)} custom-call(f32[376,128]{1,0:T(8,128)S(1)} %collective-permute-done.10.refs_0_, f32[376,128]{1,0:T(8,128)S(1)} %collective-permute-done.11.refs_1_, f32[8,128,640]{2,1,0:T(8,128)S(1)} %grid.12.refs_2_), custom_call_target="tpu_custom_call", output_to_operand_aliasing={{}: (2, {})} | custom-call | flops 1342177280 | bytes 96256 | tf_op jit(solution)/shard_map/grid/pallas_call | solution.py:190
  25.1 0.0 collective-permute-done.2.refs_0_
  25.1 2.4 %collective-permute-start.3 = (f32[376,128]{1,0:T(8,128)S(1)}, f32[376,128]{1,0:T(8,128)S(1)}, u32[]{:S(2)}, u32[]{:S(2)}) collective-permute-start(f32[376,128]{1,0:T(8,128)S(1)} %collective-permute-done.2.refs_0_), channel_id=1, source_target_pairs={{0,4},{5,1},{4,8},{9,5},{8,12},{13,9},{12,14},{15,13},{14,10},{11,... | collective-permute-start | bytes 577544 | tf_op jit(solution)/shard_map/ppermute | solution.py:283
  27.6 0.0 collective-permute-done.6.refs_1_
  27.6 0.0 collective-permute-start.7
  27.6 1.1 %grid.14.refs_2_ = f32[8,128,640]{2,1,0:T(8,128)S(1)} custom-call(f32[376,128]{1,0:T(8,128)S(1)} %collective-permute-done.2.refs_0_, f32[376,128]{1,0:T(8,128)S(1)} %collective-permute-done.6.refs_1_, f32[8,128,640]{2,1,0:T(8,128)S(1)} %grid.13.refs_2_), custom_call_target="tpu_custom_call", output_to_operand_aliasing={{}: (2, {})} | custom-call | flops 1342177280 | bytes 96256 | tf_op jit(solution)/shard_map/grid/pallas_call | solution.py:190
  28.6 0.4 %collective-permute-done.12.refs_0_ = f32[376,128]{1,0:T(8,128)S(1)} collective-permute-done((f32[376,128]{1,0:T(8,128)S(1)}, f32[376,128]{1,0:T(8,128)S(1)}, u32[]{:S(2)}, u32[]{:S(2)}) %collective-permute-start.12) | collective-permute-done | bytes 192544 | tf_op jit(solution)/shard_map/ppermute | solution.py:283
  29.0 1.4 %collective-permute-done.13.refs_1_ = f32[376,128]{1,0:T(8,128)S(1)} collective-permute-done((f32[376,128]{1,0:T(8,128)S(1)}, f32[376,128]{1,0:T(8,128)S(1)}, u32[]{:S(2)}, u32[]{:S(2)}) %collective-permute-start.13) | collective-permute-done | bytes 192544 | tf_op jit(solution)/shard_map/ppermute | solution.py:283
  30.4 2.1 %grid.15.refs_2_ = f32[8,128,640]{2,1,0:T(8,128)S(1)} custom-call(f32[376,128]{1,0:T(8,128)S(1)} %collective-permute-done.12.refs_0_, f32[376,128]{1,0:T(8,128)S(1)} %collective-permute-done.13.refs_1_, f32[8,128,640]{2,1,0:T(8,128)S(1)} %grid.14.refs_2_), custom_call_target="tpu_custom_call", output_to_operand_aliasing={{}: (2, {})} | custom-call | flops 1342177280 | bytes 96256 | tf_op jit(solution)/shard_map/grid/pallas_call | solution.py:190
  32.5 0.0 collective-permute-done.3.refs_0_
  32.5 2.4 %collective-permute-done.7.refs_1_ = f32[376,128]{1,0:T(8,128)S(1)} collective-permute-done((f32[376,128]{1,0:T(8,128)S(1)}, f32[376,128]{1,0:T(8,128)S(1)}, u32[]{:S(2)}, u32[]{:S(2)}) %collective-permute-start.7) | collective-permute-done | bytes 192544 | tf_op jit(solution)/shard_map/ppermute | solution.py:283
  34.9 0.7 %grid.16 = (f32[8,128,640]{2,1,0:T(8,128)S(1)}, f32[16,128]{1,0:T(8,128)S(1)}) custom-call(f32[376,128]{1,0:T(8,128)S(1)} %collective-permute-done.3.refs_0_, f32[376,128]{1,0:T(8,128)S(1)} %collective-permute-done.7.refs_1_, f32[8,128,640]{2,1,0:T(8,128)S(1)} %grid.15.refs_2_), custom_call_target="tpu_custom_call", output_to_operand_aliasing={{0}: (2, {})} | custom-call | flops 268435456 | bytes 96256 | tf_op jit(solution)/shard_map/grid/pallas_call | solution.py:190
  35.5 2.1 %collective-permute-start.14 = (f32[16,128]{1,0:T(8,128)S(1)}, f32[16,128]{1,0:T(8,128)S(1)}, u32[]{:S(2)}, u32[]{:S(2)}) collective-permute-start(f32[16,128]{1,0:T(8,128)S(1)} %get-tuple-element.30.mine_ref), channel_id=1, source_target_pairs={{0,1},{1,0},{2,3},{3,2},{4,5},{5,4},{6,7},{7,6},{8,9},{9,8},{10,11... | collective-permute-start | bytes 24584 | tf_op jit(solution)/shard_map/ppermute | solution.py:338
  37.7 0.0 copy-start
  37.7 0.9 %grid.17.acc_ref = f32[8,128,640]{2,1,0:T(8,128)S(1)} custom-call(f32[376,128]{1,0:T(8,128)S(1)} %collective-permute-done.3.refs_0_, f32[376,128]{1,0:T(8,128)S(1)} %collective-permute-done.7.refs_1_, f32[8,128,640]{2,1,0:T(8,128)S(1)} %get-tuple-element.29.refs_2_), custom_call_target="tpu_custom_call", output_to_operand_aliasing={{}: (2, {})} | custom-call | flops 1073741824 | bytes 96256 | tf_op jit(solution)/shard_map/grid/pallas_call | solution.py:190
  38.6 0.0 collective-permute-done.14.other_ref
  38.6 0.1 copy-done
  38.7 1.6 %image.1 = f32[2,2,2,32,256]{4,3,2,1,0:T(8,128)} custom-call(f32[8,128,640]{2,1,0:T(8,128)S(1)} %grid.17.acc_ref, f32[16,128]{1,0:T(8,128)S(1)} %get-tuple-element.30.mine_ref, f32[16,128]{1,0:T(8,128)S(1)} %collective-permute-done.14.other_ref, bf16[128,512]{1,0:T(8,128)(2,1)S(1)} %dynamic-slice_bitcast_fusion.row_ref, bf16[256,1024]{1,0:T(8,128)(2,1)S(1)} %copy-done), custom_call_target="tpu_custom_call" | custom-call | tf_op jit(solution)/shard_map/image/pallas_call | solution.py:243
Async XLA Ops:
  1.9 5.8 %collective-permute-start = (f32[376,128]{1,0:T(8,128)S(1)}, f32[376,128]{1,0:T(8,128)S(1)}, u32[]{:S(2)}, u32[]{:S(2)}) collective-permute-start(f32[376,128]{1,0:T(8,128)S(1)} %get-tuple-element.18.refs_0_), channel_id=1, source_target_pairs={{0,4},{5,1},{4,8},{9,5},{8,12},{13,9},{12,14},{15,13},{14,10},{11,... | collective-permute-start | bytes 577544 | tf_op jit(solution)/shard_map/ppermute | solution.py:283
  4.0 6.8 %collective-permute-start.4 = (f32[376,128]{1,0:T(8,128)S(1)}, f32[376,128]{1,0:T(8,128)S(1)}, u32[]{:S(2)}, u32[]{:S(2)}) collective-permute-start(f32[376,128]{1,0:T(8,128)S(1)} %get-tuple-element.19.refs_2_), channel_id=1, source_target_pairs={{4,0},{1,5},{8,4},{5,9},{12,8},{9,13},{14,12},{13,15},{10,14},{15,... | collective-permute-start | bytes 577544 | tf_op jit(solution)/shard_map/ppermute | solution.py:283
  4.1 8.7 %collective-permute-start.8 = (f32[376,128]{1,0:T(8,128)S(1)}, f32[376,128]{1,0:T(8,128)S(1)}, u32[]{:S(2)}, u32[]{:S(2)}) collective-permute-start(f32[376,128]{1,0:T(8,128)S(1)} %get-tuple-element.19.refs_2_), channel_id=1, source_target_pairs={{0,4},{5,1},{4,8},{9,5},{8,12},{13,9},{12,14},{15,13},{14,10},{11,... | collective-permute-start | bytes 577544 | tf_op jit(solution)/shard_map/ppermute | solution.py:283
  5.5 9.4 %collective-permute-start.9 = (f32[376,128]{1,0:T(8,128)S(1)}, f32[376,128]{1,0:T(8,128)S(1)}, u32[]{:S(2)}, u32[]{:S(2)}) collective-permute-start(f32[376,128]{1,0:T(8,128)S(1)} %get-tuple-element.18.refs_0_), channel_id=1, source_target_pairs={{4,0},{1,5},{8,4},{5,9},{12,8},{9,13},{14,12},{13,15},{10,14},{15,... | collective-permute-start | bytes 577544 | tf_op jit(solution)/shard_map/ppermute | solution.py:283
  7.7 9.8 %collective-permute-start.1 = (f32[376,128]{1,0:T(8,128)S(1)}, f32[376,128]{1,0:T(8,128)S(1)}, u32[]{:S(2)}, u32[]{:S(2)}) collective-permute-start(f32[376,128]{1,0:T(8,128)S(1)} %collective-permute-done.refs_0_), channel_id=1, source_target_pairs={{0,4},{5,1},{4,8},{9,5},{8,12},{13,9},{12,14},{15,13},{14,10},{11,... | collective-permute-start | bytes 577544 | tf_op jit(solution)/shard_map/ppermute | solution.py:283
  10.8 8.6 %collective-permute-start.5 = (f32[376,128]{1,0:T(8,128)S(1)}, f32[376,128]{1,0:T(8,128)S(1)}, u32[]{:S(2)}, u32[]{:S(2)}) collective-permute-start(f32[376,128]{1,0:T(8,128)S(1)} %collective-permute-done.4.refs_1_), channel_id=1, source_target_pairs={{4,0},{1,5},{8,4},{5,9},{12,8},{9,13},{14,12},{13,15},{10,14},{15,... | collective-permute-start | bytes 577544 | tf_op jit(solution)/shard_map/ppermute | solution.py:283
  14.9 5.2 %collective-permute-start.10 = (f32[376,128]{1,0:T(8,128)S(1)}, f32[376,128]{1,0:T(8,128)S(1)}, u32[]{:S(2)}, u32[]{:S(2)}) collective-permute-start(f32[376,128]{1,0:T(8,128)S(1)} %collective-permute-done.8.refs_0_), channel_id=1, source_target_pairs={{0,4},{5,1},{4,8},{9,5},{8,12},{13,9},{12,14},{15,13},{14,10},{11,... | collective-permute-start | bytes 577544 | tf_op jit(solution)/shard_map/ppermute | solution.py:283
  16.2 6.6 %collective-permute-start.11 = (f32[376,128]{1,0:T(8,128)S(1)}, f32[376,128]{1,0:T(8,128)S(1)}, u32[]{:S(2)}, u32[]{:S(2)}) collective-permute-start(f32[376,128]{1,0:T(8,128)S(1)} %collective-permute-done.9.refs_1_), channel_id=1, source_target_pairs={{4,0},{1,5},{8,4},{5,9},{12,8},{9,13},{14,12},{13,15},{10,14},{15,... | collective-permute-start | bytes 577544 | tf_op jit(solution)/shard_map/ppermute | solution.py:283
  17.6 7.5 %collective-permute-start.2 = (f32[376,128]{1,0:T(8,128)S(1)}, f32[376,128]{1,0:T(8,128)S(1)}, u32[]{:S(2)}, u32[]{:S(2)}) collective-permute-start(f32[376,128]{1,0:T(8,128)S(1)} %collective-permute-done.1.refs_0_), channel_id=1, source_target_pairs={{0,4},{5,1},{4,8},{9,5},{8,12},{13,9},{12,14},{15,13},{14,10},{11,... | collective-permute-start | bytes 577544 | tf_op jit(solution)/shard_map/ppermute | solution.py:283
  19.4 8.1 %collective-permute-start.6 = (f32[376,128]{1,0:T(8,128)S(1)}, f32[376,128]{1,0:T(8,128)S(1)}, u32[]{:S(2)}, u32[]{:S(2)}) collective-permute-start(f32[376,128]{1,0:T(8,128)S(1)} %collective-permute-done.5.refs_1_), channel_id=1, source_target_pairs={{4,0},{1,5},{8,4},{5,9},{12,8},{9,13},{14,12},{13,15},{10,14},{15,... | collective-permute-start | bytes 577544 | tf_op jit(solution)/shard_map/ppermute | solution.py:283
  22.8 6.2 %collective-permute-start.12 = (f32[376,128]{1,0:T(8,128)S(1)}, f32[376,128]{1,0:T(8,128)S(1)}, u32[]{:S(2)}, u32[]{:S(2)}) collective-permute-start(f32[376,128]{1,0:T(8,128)S(1)} %collective-permute-done.10.refs_0_), channel_id=1, source_target_pairs={{0,4},{5,1},{4,8},{9,5},{8,12},{13,9},{12,14},{15,13},{14,10},{11,... | collective-permute-start | bytes 577544 | tf_op jit(solution)/shard_map/ppermute | solution.py:283
  23.9 6.5 %collective-permute-start.13 = (f32[376,128]{1,0:T(8,128)S(1)}, f32[376,128]{1,0:T(8,128)S(1)}, u32[]{:S(2)}, u32[]{:S(2)}) collective-permute-start(f32[376,128]{1,0:T(8,128)S(1)} %collective-permute-done.11.refs_1_), channel_id=1, source_target_pairs={{4,0},{1,5},{8,4},{5,9},{12,8},{9,13},{14,12},{13,15},{10,14},{15,... | collective-permute-start | bytes 577544 | tf_op jit(solution)/shard_map/ppermute | solution.py:283
  25.1 7.4 %collective-permute-start.3 = (f32[376,128]{1,0:T(8,128)S(1)}, f32[376,128]{1,0:T(8,128)S(1)}, u32[]{:S(2)}, u32[]{:S(2)}) collective-permute-start(f32[376,128]{1,0:T(8,128)S(1)} %collective-permute-done.2.refs_0_), channel_id=1, source_target_pairs={{0,4},{5,1},{4,8},{9,5},{8,12},{13,9},{12,14},{15,13},{14,10},{11,... | collective-permute-start | bytes 577544 | tf_op jit(solution)/shard_map/ppermute | solution.py:283
  27.6 7.3 %collective-permute-start.7 = (f32[376,128]{1,0:T(8,128)S(1)}, f32[376,128]{1,0:T(8,128)S(1)}, u32[]{:S(2)}, u32[]{:S(2)}) collective-permute-start(f32[376,128]{1,0:T(8,128)S(1)} %collective-permute-done.6.refs_1_), channel_id=1, source_target_pairs={{4,0},{1,5},{8,4},{5,9},{12,8},{9,13},{14,12},{13,15},{10,14},{15,... | collective-permute-start | bytes 577544 | tf_op jit(solution)/shard_map/ppermute | solution.py:283
  35.5 3.1 %collective-permute-start.14 = (f32[16,128]{1,0:T(8,128)S(1)}, f32[16,128]{1,0:T(8,128)S(1)}, u32[]{:S(2)}, u32[]{:S(2)}) collective-permute-start(f32[16,128]{1,0:T(8,128)S(1)} %get-tuple-element.30.mine_ref), channel_id=1, source_target_pairs={{0,1},{1,0},{2,3},{3,2},{4,5},{5,4},{6,7},{7,6},{8,9},{9,8},{10,11... | collective-permute-start | bytes 24584 | tf_op jit(solution)/shard_map/ppermute | solution.py:338
  37.7 1.0 %copy-start = (bf16[256,1024]{1,0:T(8,128)(2,1)S(1)}, bf16[256,1024]{1,0:T(8,128)(2,1)}, u32[]{:S(2)}) copy-start(bf16[256,1024]{1,0:T(8,128)(2,1)} %constant.17.clone.col_ref) | copy-start | bytes 1572868
